TPU v7x, 32 devices: a whole 2x2x4 slice. The times are simulated.
32 devices in a mesh: segment: 2 (over y), lon: 4 (over x, core), lat: 4 (over z).
Axes of the slice: x: 2, y: 2, z: 4, core: 2. Of those that a mesh axis runs over, the one named last changes fastest.
Arguments:
- latents: bfloat16 [2, 24, 48, 1024], P(None, 'lat', 'lon'), may hold values from -48 to 48
- land_mask: int32 [24, 48], P('lat', 'lon'), may hold values 0 or 1
- land_embed: bfloat16 [1024], replicated, may hold values from -6 to 6
- qkv_weight: bfloat16 [2, 1024, 3072], P('segment'), may hold values from -0.25625 to 0.25625
- out_weight: bfloat16 [2, 1024, 1024], P('segment'), may hold values from -0.5625 to 0.5625
- norm_gain: float32 [2, 1024], replicated, may hold values from 0.5 to 1.5
- offsets: int32 [2, 2], replicated, may hold values from 0 to 11, as said below
Outputs:
- sections: bfloat16 [2, 2, 24, 48, 1024], P('segment', None, 'lat', 'lon')
Inputs may be any that keep to these rules, and one draw needn't show every extreme that they name: offsets[s, 0] lies in 0 to 5 and offsets[s, 1] in 0 to 11; one of the two sections has offsets[s, 0] = 5 and offsets[s, 1] = 11.
All inputs are finite; a program needn't handle non-finite values. No bound on the sum of `land_mask` on one device may be relied on, other than what follows from the above.
Results may differ from a plain program's by a relative error of at most 0.015.
Values may be sent and summed in bfloat16 or wider, within the bound.
A program may use at most 64 MiB of HBM per device.

v0:
```python
import math

import jax
import jax.numpy as jnp
from jax import lax
from jax.sharding import PartitionSpec as P

HEADS = 16
WLAT = 6
WLON = 12


def shifted(block, axis, distance):
    devices = range(lax.axis_size(axis))
    route = [((i - distance) % len(devices), i) for i in devices]
    return lax.ppermute(block, axis, route)


def from_behind(block, axis, distance):
    devices = range(lax.axis_size(axis))
    route = [(i - distance, i) for i in devices if i - distance in devices]
    return lax.ppermute(block, axis, route)


def window_cells(field):
    block_count, row_count, column_count, width = field.shape
    parted = field.reshape(block_count, row_count // WLAT, WLAT, column_count // WLON, WLON, width)
    parted = parted.transpose(0, 1, 3, 2, 4, 5)
    return parted.reshape(-1, WLAT * WLON, width)


def grid_cells(cells, block_count, row_count, column_count):
    width = cells.shape[-1]
    parted = cells.reshape(block_count, row_count // WLAT, column_count // WLON, WLAT, WLON, width)
    parted = parted.transpose(0, 1, 3, 2, 4, 5)
    return parted.reshape(block_count, row_count, column_count, width)


def attend(rolled, wqkv, wout, gain, lat_offset):
    block_count, row_count, column_count, width = rolled.shape
    head_size = width // HEADS
    cell_count = WLAT * WLON
    cells = window_cells(rolled)
    window_count = cells.shape[0]
    flat = cells.reshape(-1, width)
    packed = jnp.dot(flat, wqkv, preferred_element_type=jnp.float32).astype(jnp.bfloat16)
    packed = packed.reshape(window_count, cell_count, 3, HEADS, head_size)
    queries = packed[:, :, 0]
    keys = packed[:, :, 1]
    values = packed[:, :, 2]
    scores = jnp.einsum(
        "nqhd,nkhd->nhqk", queries, keys, preferred_element_type=jnp.float32
    ) / math.sqrt(head_size)
    total_rows = row_count * lax.axis_size("lat")
    row_global = lax.axis_index("lat") * row_count + jnp.arange(row_count, dtype=jnp.int32)
    wrapped = row_global + lat_offset >= total_rows
    row_windows = row_count // WLAT
    col_windows = column_count // WLON
    flags = jnp.broadcast_to(
        wrapped.reshape(row_windows, 1, WLAT, 1), (row_windows, col_windows, WLAT, WLON)
    )
    flags = flags.reshape(row_windows * col_windows, cell_count)
    allowed = flags[:, :, None] == flags[:, None, :]
    scores = scores.reshape(block_count, row_windows * col_windows, HEADS, cell_count, cell_count)
    scores = jnp.where(allowed[None, :, None], scores, -1e30)
    probs = jax.nn.softmax(scores, axis=-1).astype(jnp.bfloat16)
    probs = probs.reshape(window_count, HEADS, cell_count, cell_count)
    attended = jnp.einsum("nhqk,nkhd->nqhd", probs, values, preferred_element_type=jnp.float32)
    attended = attended.astype(jnp.bfloat16).reshape(-1, width)
    projected = jnp.dot(attended, wout, preferred_element_type=jnp.float32)
    centered = projected - jnp.mean(projected, axis=-1, keepdims=True)
    variance = jnp.mean(centered * centered, axis=-1, keepdims=True)
    branch = centered * lax.rsqrt(variance + 1e-05) * gain
    summed = (flat.astype(jnp.float32) + branch).astype(jnp.bfloat16)
    return grid_cells(
        summed.reshape(window_count, cell_count, width), block_count, row_count, column_count
    )


def section(field, wqkv, wout, gain, lat_offset, lon_offset):
    row_count = field.shape[1]
    column_count = field.shape[2]
    east_cols = shifted(field, "lon", -1)
    wide_grid = jnp.concatenate([field, east_cols], axis=2)
    rolled = lax.dynamic_slice_in_dim(wide_grid, lon_offset, column_count, 2)
    south_rows = shifted(rolled, "lat", -1)
    tall_grid = jnp.concatenate([rolled, south_rows], axis=1)
    rolled = lax.dynamic_slice_in_dim(tall_grid, lat_offset, row_count, 1)
    summed = attend(rolled, wqkv, wout, gain, lat_offset)
    north_rows = shifted(summed, "lat", 1)
    tall_back = jnp.concatenate([north_rows, summed], axis=1)
    unrolled = lax.dynamic_slice_in_dim(tall_back, WLAT - lat_offset, row_count, 1)
    west_cols = shifted(unrolled, "lon", 1)
    wide_back = jnp.concatenate([west_cols, unrolled], axis=2)
    return lax.dynamic_slice_in_dim(wide_back, WLON - lon_offset, column_count, 2)


def pass_on(field):
    return from_behind(field, "segment", 1)


def body(latents, land_mask, land_embed, qkv_weight, out_weight, norm_gain, offsets):
    segment_index = lax.axis_index("segment")
    land_term = land_mask.astype(jnp.float32)[None, :, :, None] * land_embed.astype(jnp.float32)
    seeded = (latents.astype(jnp.float32) + land_term).astype(jnp.bfloat16)
    wqkv = qkv_weight[0]
    wout = out_weight[0]
    gain = lax.dynamic_index_in_dim(norm_gain, segment_index, 0, False)
    own_offsets = lax.dynamic_index_in_dim(offsets, segment_index, 0, False)
    lat_offset = own_offsets[0]
    lon_offset = own_offsets[1]

    def apply_section(field):
        return section(field, wqkv, wout, gain, lat_offset, lon_offset)

    first_pass = apply_section(seeded)
    second_pass = apply_section(pass_on(first_pass))
    merged = jnp.where(segment_index == 0, first_pass, second_pass)
    return merged[None]


def solution(mesh):
    return jax.shard_map(
        body,
        mesh=mesh,
        in_specs=(
            P(None, "lat", "lon", None),
            P("lat", "lon"),
            P(),
            P("segment", None, None),
            P("segment", None, None),
            P(),
            P(),
        ),
        out_specs=P("segment", None, "lat", "lon", None),
        check_vma=False,
    )
```

profile of v0, /device:TPU:4, one launch (start us, length us, event | category | flops | bytes accessed | tf_op | source)
XLA Modules:
  0.0 140.8 jit_solution(826937751672605665)
XLA Ops:
  0.0 0.8 convert_element_type.51
  0.8 0.7 convert_element_type.52
  1.6 1.3 add_convert_fusion.2
  2.9 1.0 collective-permute-start
  3.9 0.6 fusion.58
  6.9 0.7 add_compare_fusion
  9.0 0.8 fusion.41
  9.7 3.7 %collective-permute-start.1 = (bf16[2,6,12,1024]{3,0,2,1:T(2,128)(2,1)S(1)}, bf16[2,6,12,1024]{3,0,2,1:T(2,128)(2,1)S(1)}, u32[]{:S(2)}, u32[]{:S(2)}) collective-permute-start(bf16[2,6,12,1024]{3,0,2,1:T(2,128)(2,1)S(1)} %fusion.41), channel_id=1, source_target_pairs={{1,0},{2,1},{3,2},{0,3},{5,4},{6,5},{7,6},{4,7},{9,8},{10,9},{11,1... | collective-permute-start | bytes 884744 | tf_op jit(solution)/shard_map/ppermute | solution.py:16
  13.5 6.3 %collective-permute-done.1 = bf16[2,6,12,1024]{3,0,2,1:T(2,128)(2,1)S(1)} collective-permute-done((bf16[2,6,12,1024]{3,0,2,1:T(2,128)(2,1)S(1)}, bf16[2,6,12,1024]{3,0,2,1:T(2,128)(2,1)S(1)}, u32[]{:S(2)}, u32[]{:S(2)}) %collective-permute-start.1) | collective-permute-done | bytes 294944 | tf_op jit(solution)/shard_map/ppermute | solution.py:16
  19.8 0.7 fusion.40
  20.7 3.9 %fusion.6 = bf16[144,3072]{1,0:T(8,128)(2,1)S(1)} fusion(bf16[144,1024]{1,0:T(8,128)(2,1)S(1)} %reshape_reshape_transpose_reshape.6, bf16[1,1024,3072]{2,1,0:T(8,128)(2,1)} %param.10), kind=kOutput, calls=%fused_computation.6 | convolution fusion | flops 906412032 | bytes 7471104 | tf_op jit(solution)/shard_map/dot_general | solution.py:46
  24.6 2.1 %reshape.141 = bf16[2,72,3,16,64]{4,3,2,1,0:T(8,128)(2,1)} reshape(bf16[144,3072]{1,0:T(8,128)(2,1)S(1)} %fusion.6) | data formatting | bytes 1769472 | tf_op jit(solution)/shard_map/reshape | solution.py:47
  26.7 2.8 %fusion.57 = (bf16[2,72,1,16,64]{4,3,2,1,0:T(8,128)(2,1)S(1)}, bf16[2,72,1,16,64]{4,3,2,1,0:T(8,128)(2,1)}, bf16[2,72,1,16,64]{4,3,2,1,0:T(8,128)(2,1)}) fusion(bf16[2,72,3,16,64]{4,3,2,1,0:T(8,128)(2,1)} %reshape.141), kind=kLoop, calls=%fused_computation.81 | loop fusion | bytes 1769472 | tf_op jit(solution)/shard_map/slice | solution.py:50
  29.4 1.5 %copy.37 = bf16[2,72,1,16,64]{1,4,3,0,2:T(8,128)(2,1)S(1)} copy(bf16[2,72,1,16,64]{4,3,2,1,0:T(8,128)(2,1)} %get-tuple-element.9) | data formatting | bytes 589824
  31.0 2.3 %copy.38 = bf16[2,72,1,16,64]{1,4,3,0,2:T(8,128)(2,1)} copy(bf16[2,72,1,16,64]{4,3,2,1,0:T(8,128)(2,1)} %get-tuple-element.10) | data formatting | bytes 589824
  33.3 1.7 %fusion.59 = f32[2,16,72]{2,1,0:T(8,128)S(1)} fusion(pred[72,72]{0,1:T(8,128)(4,1)S(1)} %broadcast_compare_fusion, bf16[2,72,1,16,64]{1,4,3,0,2:T(8,128)(2,1)} %copy.38, bf16[2,72,1,16,64]{1,4,3,0,2:T(8,128)(2,1)S(1)} %copy.37), kind=kOutput, calls=%fused_computation.83 | convolution fusion | flops 21897288 | bytes 604224 | tf_op jit(solution)/shard_map/sub | solution.py:66
  35.1 2.6 %fusion.21 = f32[2,16,72,72]{2,3,1,0:T(8,128)} fusion(pred[72,72]{0,1:T(8,128)(4,1)S(1)} %broadcast_compare_fusion, bf16[2,72,1,16,64]{1,4,3,0,2:T(8,128)(2,1)} %copy.38, bf16[2,72,1,16,64]{1,4,3,0,2:T(8,128)(2,1)S(1)} %copy.37), kind=kOutput, calls=%fused_computation.19 | convolution fusion | flops 21565440 | bytes 1258560 | tf_op jit(solution)/shard_map/nqhd,nkhd->nhqk/dot_general | solution.py:51
  37.6 0.5 copy.36
  38.2 2.9 %fusion.22 = bf16[2,72,16,64]{1,3,2,0:T(8,128)(2,1)} fusion(f32[2,16,72]{2,1,0:T(8,128)S(1)} %fusion.59, bf16[2,72,1,16,64]{1,4,3,0,2:T(8,128)(2,1)S(1)} %copy.36, f32[2,16,72,72]{2,3,1,0:T(8,128)} %fusion.21), kind=kOutput, calls=%fused_computation.22 | convolution fusion | flops 21881160 | bytes 1262592 | tf_op jit(solution)/shard_map/nhqk,nkhd->nqhd/dot_general | solution.py:68
  41.1 1.5 %copy.27 = bf16[2,72,16,64]{3,2,1,0:T(8,128)(2,1)S(1)} copy(bf16[2,72,16,64]{1,3,2,0:T(8,128)(2,1)} %fusion.22) | data formatting | bytes 589824 | tf_op jit(solution)/shard_map/convert_element_type | solution.py:69
  42.6 0.4 reshape.142
  43.0 0.6 fusion.64
  44.1 0.5 collective-permute-start.2
  45.9 10.9 %collective-permute-done.2 = bf16[2,6,12,1024]{3,2,1,0:T(8,128)(2,1)S(1)} collective-permute-done((bf16[2,6,12,1024]{3,2,1,0:T(8,128)(2,1)S(1)}, bf16[2,6,12,1024]{3,2,1,0:T(8,128)(2,1)S(1)}, u32[]{:S(2)}, u32[]{:S(2)}) %collective-permute-start.2) | collective-permute-done | bytes 294944 | tf_op jit(solution)/shard_map/ppermute | solution.py:16
  58.2 6.1 %collective-permute-done.3 = bf16[2,6,12,1024]{3,2,1,0:T(8,128)(2,1)S(1)} collective-permute-done((bf16[2,6,12,1024]{3,2,1,0:T(8,128)(2,1)S(1)}, bf16[2,6,12,1024]{3,2,1,0:T(8,128)(2,1)S(1)}, u32[]{:S(2)}, u32[]{:S(2)}) %collective-permute-start.3) | collective-permute-done | bytes 294944 | tf_op jit(solution)/shard_map/ppermute | solution.py:16
  64.3 0.3 fusion.36
  64.6 1.3 collective-permute-start.4
  65.9 11.6 %collective-permute-done.4 = bf16[2,6,12,1024]{3,2,1,0:T(8,128)(2,1)S(1)} collective-permute-done((bf16[2,6,12,1024]{3,2,1,0:T(8,128)(2,1)S(1)}, bf16[2,6,12,1024]{3,2,1,0:T(8,128)(2,1)S(1)}, u32[]{:S(2)}, u32[]{:S(2)}) %collective-permute-start.4) | collective-permute-done | bytes 294944 | tf_op jit(solution)/shard_map/ppermute | solution.py:22
  77.5 5.3 %collective-permute-done.5 = bf16[2,6,12,1024]{3,2,1,0:T(8,128)(2,1)S(1)} collective-permute-done((bf16[2,6,12,1024]{3,2,1,0:T(8,128)(2,1)S(1)}, bf16[2,6,12,1024]{3,2,1,0:T(8,128)(2,1)S(1)}, u32[]{:S(2)}, u32[]{:S(2)}) %collective-permute-start.5) | collective-permute-done | bytes 294944 | tf_op jit(solution)/shard_map/ppermute | solution.py:16
  82.8 0.3 fusion.35
  83.2 2.0 %collective-permute-start.6 = (bf16[2,6,12,1024]{3,2,1,0:T(8,128)(2,1)S(1)}, bf16[2,6,12,1024]{3,2,1,0:T(8,128)(2,1)S(1)}, u32[]{:S(2)}, u32[]{:S(2)}) collective-permute-start(bf16[2,6,12,1024]{3,2,1,0:T(8,128)(2,1)S(1)} %fusion.35), channel_id=1, source_target_pairs={{1,0},{2,1},{3,2},{0,3},{5,4},{6,5},{7,6},{4,7},{9,8},{10,9},{11,1... | collective-permute-start | bytes 884744 | tf_op jit(solution)/shard_map/ppermute | solution.py:16
  85.1 10.2 %collective-permute-done.6 = bf16[2,6,12,1024]{3,2,1,0:T(8,128)(2,1)S(1)} collective-permute-done((bf16[2,6,12,1024]{3,2,1,0:T(8,128)(2,1)S(1)}, bf16[2,6,12,1024]{3,2,1,0:T(8,128)(2,1)S(1)}, u32[]{:S(2)}, u32[]{:S(2)}) %collective-permute-start.6) | collective-permute-done | bytes 294944 | tf_op jit(solution)/shard_map/ppermute | solution.py:16
  95.6 3.9 %fusion.9 = bf16[144,3072]{1,0:T(8,128)(2,1)S(1)} fusion(bf16[144,1024]{1,0:T(8,128)(2,1)S(1)} %reshape_reshape_transpose_reshape.7, bf16[1,1024,3072]{2,1,0:T(8,128)(2,1)} %param.10), kind=kOutput, calls=%fused_computation.7 | convolution fusion | flops 906412032 | bytes 7471104 | tf_op jit(solution)/shard_map/dot_general | solution.py:46
  99.5 2.1 %reshape.143 = bf16[2,72,3,16,64]{4,3,2,1,0:T(8,128)(2,1)} reshape(bf16[144,3072]{1,0:T(8,128)(2,1)S(1)} %fusion.9) | data formatting | bytes 1769472 | tf_op jit(solution)/shard_map/reshape | solution.py:47
  101.6 2.8 %fusion.56 = (bf16[2,72,1,16,64]{4,3,2,1,0:T(8,128)(2,1)S(1)}, bf16[2,72,1,16,64]{4,3,2,1,0:T(8,128)(2,1)}, bf16[2,72,1,16,64]{4,3,2,1,0:T(8,128)(2,1)}) fusion(bf16[2,72,3,16,64]{4,3,2,1,0:T(8,128)(2,1)} %reshape.143), kind=kLoop, calls=%fused_computation.80 | loop fusion | bytes 1769472 | tf_op jit(solution)/shard_map/slice | solution.py:50
  104.3 1.5 %copy.40 = bf16[2,72,1,16,64]{1,4,3,0,2:T(8,128)(2,1)S(1)} copy(bf16[2,72,1,16,64]{4,3,2,1,0:T(8,128)(2,1)} %get-tuple-element.6) | data formatting | bytes 589824
  105.9 2.3 %copy.41 = bf16[2,72,1,16,64]{1,4,3,0,2:T(8,128)(2,1)} copy(bf16[2,72,1,16,64]{4,3,2,1,0:T(8,128)(2,1)} %get-tuple-element.7) | data formatting | bytes 589824
  108.2 1.7 %fusion.65 = f32[2,16,72]{2,1,0:T(8,128)S(1)} fusion(pred[72,72]{0,1:T(8,128)(4,1)S(1)} %broadcast_compare_fusion, bf16[2,72,1,16,64]{1,4,3,0,2:T(8,128)(2,1)} %copy.41, bf16[2,72,1,16,64]{1,4,3,0,2:T(8,128)(2,1)S(1)} %copy.40), kind=kOutput, calls=%fused_computation.85 | convolution fusion | flops 21897288 | bytes 604224 | tf_op jit(solution)/shard_map/sub | solution.py:66
  109.9 2.6 %fusion.20 = f32[2,16,72,72]{2,3,1,0:T(8,128)} fusion(pred[72,72]{0,1:T(8,128)(4,1)S(1)} %broadcast_compare_fusion, bf16[2,72,1,16,64]{1,4,3,0,2:T(8,128)(2,1)} %copy.41, bf16[2,72,1,16,64]{1,4,3,0,2:T(8,128)(2,1)S(1)} %copy.40), kind=kOutput, calls=%fused_computation.17 | convolution fusion | flops 21565440 | bytes 1258560 | tf_op jit(solution)/shard_map/nqhd,nkhd->nhqk/dot_general | solution.py:51
  112.5 0.5 copy.39
  113.1 2.9 %fusion.23 = bf16[2,72,16,64]{1,3,2,0:T(8,128)(2,1)} fusion(f32[2,16,72]{2,1,0:T(8,128)S(1)} %fusion.65, bf16[2,72,1,16,64]{1,4,3,0,2:T(8,128)(2,1)S(1)} %copy.39, f32[2,16,72,72]{2,3,1,0:T(8,128)} %fusion.20), kind=kOutput, calls=%fused_computation.23 | convolution fusion | flops 21881160 | bytes 1262592 | tf_op jit(solution)/shard_map/nhqk,nkhd->nqhd/dot_general | solution.py:68
  115.9 1.5 %copy.32 = bf16[2,72,16,64]{3,2,1,0:T(8,128)(2,1)S(1)} copy(bf16[2,72,16,64]{1,3,2,0:T(8,128)(2,1)} %fusion.23) | data formatting | bytes 589824 | tf_op jit(solution)/shard_map/convert_element_type | solution.py:69
  117.5 0.4 reshape.144
  117.9 0.6 fusion.70
  119.0 12.9 %collective-permute-done.7 = bf16[2,6,12,1024]{3,2,1,0:T(8,128)(2,1)S(1)} collective-permute-done((bf16[2,6,12,1024]{3,2,1,0:T(8,128)(2,1)S(1)}, bf16[2,6,12,1024]{3,2,1,0:T(8,128)(2,1)S(1)}, u32[]{:S(2)}, u32[]{:S(2)}) %collective-permute-start.7) | collective-permute-done | bytes 294944 | tf_op jit(solution)/shard_map/ppermute | solution.py:16
  132.2 7.2 %collective-permute-done.8 = bf16[2,6,12,1024]{3,2,1,0:T(8,128)(2,1)S(1)} collective-permute-done((bf16[2,6,12,1024]{3,2,1,0:T(8,128)(2,1)S(1)}, bf16[2,6,12,1024]{3,2,1,0:T(8,128)(2,1)S(1)}, u32[]{:S(2)}, u32[]{:S(2)}) %collective-permute-start.8) | collective-permute-done | bytes 294944 | tf_op jit(solution)/shard_map/ppermute | solution.py:16
  139.4 0.4 fusion.34
  139.8 1.0 copy.33
  (37 shorter events, 2.3 us)
Async XLA Ops:
  0.0 43.0 %copy-start = (bf16[1,1024,1024]{2,1,0:T(8,128)(2,1)S(1)}, bf16[1,1024,1024]{2,1,0:T(8,128)(2,1)}, u32[]{:S(2)}) copy-start(bf16[1,1024,1024]{2,1,0:T(8,128)(2,1)} %param.11) | copy-start | bytes 6291460
  0.0 3.9 %copy-start.4 = (s32[2,2]{1,0:T(2,128)S(1)}, s32[2,2]{1,0:T(2,128)}, u32[]{:S(2)}) copy-start(s32[2,2]{1,0:T(2,128)} %param.13) | copy-start | bytes 52
  0.0 13.4 %copy-start.3 = (f32[2,1024]{1,0:T(2,128)S(1)}, f32[2,1024]{1,0:T(2,128)}, u32[]{:S(2)}) copy-start(f32[2,1024]{1,0:T(2,128)} %param.12) | copy-start | bytes 24580
  2.9 6.1 %collective-permute-start = (bf16[2,6,12,1024]{3,0,2,1:T(2,128)(2,1)S(1)}, bf16[2,6,12,1024]{3,0,2,1:T(2,128)(2,1)S(1)}, u32[]{:S(2)}, u32[]{:S(2)}) collective-permute-start(bf16[2,6,12,1024]{3,0,2,1:T(2,128)(2,1)S(1)} %add_convert_fusion.2), channel_id=1, source_target_pairs={{4,0},{8,4},{12,8},{0,12},{5,1},{9,5},{13,9},{1,13},{6,2},{10,6},{... | collective-permute-start | bytes 884744 | tf_op jit(solution)/shard_map/ppermute | solution.py:16
  9.7 10.1 %collective-permute-start.1 = (bf16[2,6,12,1024]{3,0,2,1:T(2,128)(2,1)S(1)}, bf16[2,6,12,1024]{3,0,2,1:T(2,128)(2,1)S(1)}, u32[]{:S(2)}, u32[]{:S(2)}) collective-permute-start(bf16[2,6,12,1024]{3,0,2,1:T(2,128)(2,1)S(1)} %fusion.41), channel_id=1, source_target_pairs={{1,0},{2,1},{3,2},{0,3},{5,4},{6,5},{7,6},{4,7},{9,8},{10,9},{11,1... | collective-permute-start | bytes 884744 | tf_op jit(solution)/shard_map/ppermute | solution.py:16
  44.1 12.8 %collective-permute-start.2 = (bf16[2,6,12,1024]{3,2,1,0:T(8,128)(2,1)S(1)}, bf16[2,6,12,1024]{3,2,1,0:T(8,128)(2,1)S(1)}, u32[]{:S(2)}, u32[]{:S(2)}) collective-permute-start(bf16[2,6,12,1024]{3,2,1,0:T(8,128)(2,1)S(1)} %reshape_transpose_reshape_reshape.6), channel_id=1, source_target_pairs={{3,0},{0,1},{1,2},{2,3},{7,4},{4,5},{5,6},{6,7},{11,8},{8,9},{9,10... | collective-permute-start | bytes 884744 | tf_op jit(solution)/shard_map/ppermute | solution.py:16
  57.0 7.3 %collective-permute-start.3 = (bf16[2,6,12,1024]{3,2,1,0:T(8,128)(2,1)S(1)}, bf16[2,6,12,1024]{3,2,1,0:T(8,128)(2,1)S(1)}, u32[]{:S(2)}, u32[]{:S(2)}) collective-permute-start(bf16[2,6,12,1024]{3,2,1,0:T(8,128)(2,1)S(1)} %fusion.39), channel_id=1, source_target_pairs={{12,0},{0,4},{4,8},{8,12},{13,1},{1,5},{5,9},{9,13},{14,2},{2,6},{... | collective-permute-start | bytes 884744 | tf_op jit(solution)/shard_map/ppermute | solution.py:16
  64.6 30.7 %copy-start.1 = (bf16[2,6,12,1024]{3,2,1,0:T(8,128)(2,1)}, bf16[2,6,12,1024]{3,2,1,0:T(8,128)(2,1)S(1)}, u32[]{:S(2)}) copy-start(bf16[2,6,12,1024]{3,2,1,0:T(8,128)(2,1)S(1)} %fusion.36) | copy-start | bytes 884740
  64.6 12.9 %collective-permute-start.4 = (bf16[2,6,12,1024]{3,2,1,0:T(8,128)(2,1)S(1)}, bf16[2,6,12,1024]{3,2,1,0:T(8,128)(2,1)S(1)}, u32[]{:S(2)}, u32[]{:S(2)}) collective-permute-start(bf16[2,6,12,1024]{3,2,1,0:T(8,128)(2,1)S(1)} %fusion.36), channel_id=1, source_target_pairs={{0,16},{1,17},{2,18},{3,19},{4,20},{5,21},{6,22},{7,23},{8,24},{9,... | collective-permute-start | bytes 884744 | tf_op jit(solution)/shard_map/ppermute | solution.py:22
  77.5 5.3 %collective-permute-start.5 = (bf16[2,6,12,1024]{3,2,1,0:T(8,128)(2,1)S(1)}, bf16[2,6,12,1024]{3,2,1,0:T(8,128)(2,1)S(1)}, u32[]{:S(2)}, u32[]{:S(2)}) collective-permute-start(bf16[2,6,12,1024]{3,2,1,0:T(8,128)(2,1)S(1)} %collective-permute-done.4), channel_id=1, source_target_pairs={{4,0},{8,4},{12,8},{0,12},{5,1},{9,5},{13,9},{1,13},{6,2},{10,6},{... | collective-permute-start | bytes 884744 | tf_op jit(solution)/shard_map/ppermute | solution.py:16
  83.2 12.2 %collective-permute-start.6 = (bf16[2,6,12,1024]{3,2,1,0:T(8,128)(2,1)S(1)}, bf16[2,6,12,1024]{3,2,1,0:T(8,128)(2,1)S(1)}, u32[]{:S(2)}, u32[]{:S(2)}) collective-permute-start(bf16[2,6,12,1024]{3,2,1,0:T(8,128)(2,1)S(1)} %fusion.35), channel_id=1, source_target_pairs={{1,0},{2,1},{3,2},{0,3},{5,4},{6,5},{7,6},{4,7},{9,8},{10,9},{11,1... | collective-permute-start | bytes 884744 | tf_op jit(solution)/shard_map/ppermute | solution.py:16
  118.9 20.5 %copy-start.2 = (bf16[2,6,12,1024]{3,2,1,0:T(8,128)(2,1)S(1)}, bf16[2,6,12,1024]{3,2,1,0:T(8,128)(2,1)}, u32[]{:S(2)}) copy-start(bf16[2,6,12,1024]{3,2,1,0:T(8,128)(2,1)} %copy-done.1) | copy-start | bytes 884740
  119.0 13.0 %collective-permute-start.7 = (bf16[2,6,12,1024]{3,2,1,0:T(8,128)(2,1)S(1)}, bf16[2,6,12,1024]{3,2,1,0:T(8,128)(2,1)S(1)}, u32[]{:S(2)}, u32[]{:S(2)}) collective-permute-start(bf16[2,6,12,1024]{3,2,1,0:T(8,128)(2,1)S(1)} %reshape_transpose_reshape_reshape.7), channel_id=1, source_target_pairs={{3,0},{0,1},{1,2},{2,3},{7,4},{4,5},{5,6},{6,7},{11,8},{8,9},{9,10... | collective-permute-start | bytes 884744 | tf_op jit(solution)/shard_map/ppermute | solution.py:16
  132.1 7.3 %collective-permute-start.8 = (bf16[2,6,12,1024]{3,2,1,0:T(8,128)(2,1)S(1)}, bf16[2,6,12,1024]{3,2,1,0:T(8,128)(2,1)S(1)}, u32[]{:S(2)}, u32[]{:S(2)}) collective-permute-start(bf16[2,6,12,1024]{3,2,1,0:T(8,128)(2,1)S(1)} %fusion.37), channel_id=1, source_target_pairs={{12,0},{0,4},{4,8},{8,12},{13,1},{1,5},{5,9},{9,13},{14,2},{2,6},{... | collective-permute-start | bytes 884744 | tf_op jit(solution)/shard_map/ppermute | solution.py:16
where the time goes:
time: 142 us; the launch traced here: 141 us
  waiting for transfers between devices  70.5 us (50%)
  local copies, waits for them, and re-layouts  24.4 us (17%)
  matrix products  23.3 us (16%)
  starting transfers between devices  8.58 us (6%)
  other arithmetic  7.6 us (5%)
  between operations  6.37 us (4%)
    ppermute x8, waiting for transfers between devices, shifted(): return lax.ppermute(block, axis, route)  59 us
    ppermute x1, waiting for transfers between devices, from_behind(): return lax.ppermute(block, axis, route)  11.6 us
    unnamed x16, local copies, waits for them, and re-layouts  8.85 us
    dot_general x2, matrix products, attend(): jnp.dot(flat, wqkv, preferred_element_type=jnp.float32).astype(jnp.bfloat16)  7.76 us
    ppermute x8, starting transfers between devices, shifted(): return lax.ppermute(block, axis, route)  7.29 us
    dot_general x2, matrix products, attend(): jnp.einsum('nhqk,nkhd->nqhd', probs, values, preferred_element_type=jnp.f...  5.76 us
    slice x2, local copies, waits for them, and re-layouts, attend(): values = packed[:, :, 2]  5.54 us
    dot_general x2, matrix products, attend(): jnp.einsum('nqhd,nkhd->nhqk', queries, keys, preferred_element_type=jnp.f...  5.15 us
  transfers between devices with their start and end apart: 9, of which 8 were waited for; matrix products, arithmetic and copies ran while one was open for 1% of the time, Pallas kernels for 0%

commit v1 on v0

v1 whole, which is shorter than its diff:
```python
import functools
import math

import jax
import jax.numpy as jnp
from jax import lax
from jax.experimental import pallas as pl
from jax.experimental.pallas import tpu as pltpu
from jax.sharding import PartitionSpec as P

HEADS = 16
WLAT = 6
WLON = 12
HALF_LAT = WLAT // 2
HALF_LON = WLON // 2
STEPS = 4
PAIR = 128
NT = (((1,), (1,)), ((), ()))


def attend_kernel(col_code, row_code, x_ref, wq_ref, wk_ref, wv_ref, wo_ref, gain_ref, out_ref, total, *, head_size):
    step = pl.program_id(0)
    x = x_ref[...]
    q = jnp.dot(x, wq_ref[...], preferred_element_type=jnp.float32).astype(jnp.bfloat16)
    k = jnp.dot(x, wk_ref[...], preferred_element_type=jnp.float32).astype(jnp.bfloat16)
    v = jnp.dot(x, wv_ref[...], preferred_element_type=jnp.float32).astype(jnp.bfloat16)
    allowed = col_code[...] == row_code[...]
    scale = 1.0 / math.sqrt(head_size)
    first_half = lax.broadcasted_iota(jnp.int32, (x.shape[0], PAIR), 1) < head_size
    parts = []
    for pair in range(q.shape[1] // PAIR):
        columns = slice(pair * PAIR, (pair + 1) * PAIR)
        q2, k2, v2 = q[:, columns], k[:, columns], v[:, columns]
        weighted = []
        for keep in (first_half, ~first_half):
            qh = jnp.where(keep, q2, jnp.zeros_like(q2))
            scores = lax.dot_general(qh, k2, NT, preferred_element_type=jnp.float32) * scale
            scores = jnp.where(allowed, scores, -1e30)
            weights = jnp.exp(scores - jnp.max(scores, axis=-1, keepdims=True))
            inverse = 1.0 / jnp.sum(weights, axis=-1, keepdims=True)
            probs = (weights * inverse).astype(jnp.bfloat16)
            weighted.append(jnp.dot(probs, v2, preferred_element_type=jnp.float32))
        parts.append(jnp.where(first_half, weighted[0], weighted[1]).astype(jnp.bfloat16))
    attended = jnp.concatenate(parts, axis=1)
    projected = jnp.dot(attended, wo_ref[...], preferred_element_type=jnp.float32)

    @pl.when(step == 0)
    def _():
        total[...] = projected

    @pl.when(step > 0)
    def _():
        total[...] += projected

    @pl.when(step == STEPS - 1)
    def _():
        whole = total[...]
        centered = whole - jnp.mean(whole, axis=-1, keepdims=True)
        variance = jnp.mean(centered * centered, axis=-1, keepdims=True)
        branch = centered * lax.rsqrt(variance + 1e-05) * gain_ref[...]
        out_ref[...] = (x.astype(jnp.float32) + branch).astype(jnp.bfloat16)


def attend(field, codes, wqkv, wout, gain):
    width = field.shape[-1]
    flat = field.reshape(-1, width)
    cells = flat.shape[0]
    slab = width // STEPS
    head_size = width // HEADS
    full = lambda shape: pl.BlockSpec(shape, lambda p: (0, 0))
    out = pl.pallas_call(
        functools.partial(attend_kernel, head_size=head_size),
        grid=(STEPS,),
        out_shape=jax.ShapeDtypeStruct((cells, width), jnp.bfloat16),
        in_specs=[
            full((cells, 1)),
            full((1, cells)),
            full((cells, width)),
            pl.BlockSpec((width, slab), lambda p: (0, p)),
            pl.BlockSpec((width, slab), lambda p: (0, p + STEPS)),
            pl.BlockSpec((width, slab), lambda p: (0, p + 2 * STEPS)),
            pl.BlockSpec((slab, width), lambda p: (p, 0)),
            full((1, width)),
        ],
        out_specs=full((cells, width)),
        scratch_shapes=[pltpu.VMEM((cells, width), jnp.float32)],
        compiler_params=pltpu.CompilerParams(vmem_limit_bytes=24 * 1024 * 1024),
        cost_estimate=pl.CostEstimate(
            flops=8 * cells * width * width, bytes_accessed=8 * width * width, transcendentals=HEADS * cells * cells
        ),
    )(codes[:, None], codes[None, :], flat, wqkv, wqkv, wqkv, wout, gain[None, :])
    return out.reshape(field.shape)


def moved(piece, lat_steps, lon_steps):
    segments, lons, lats = (lax.axis_size(axis) for axis in ("segment", "lon", "lat"))
    place = lambda s, j, i: (s * lons + j % lons) * lats + i % lats
    route = [
        (place(s, j + lon_steps[s], i + lat_steps[s]), place(s, j, i))
        for s in range(segments)
        for j in range(lons)
        for i in range(lats)
    ]
    return lax.ppermute(piece, ("segment", "lon", "lat"), route)


def by_segment(make, steps):
    if steps[0] == steps[1]:
        return make(steps[0])
    return jnp.where(lax.axis_index("segment") == 0, make(steps[0]), make(steps[1]))


def shift_one_way(lat_steps, lon_steps, field, lat_shift, lon_shift):
    rows = lambda step: field[:, :HALF_LAT] if step > 0 else field[:, WLAT - HALF_LAT:]
    columns = lambda part: lambda step: part[:, :, :HALF_LON] if step > 0 else part[:, :, WLON - HALF_LON:]
    still = (0, 0)
    row_piece = by_segment(rows, lat_steps)
    below = moved(row_piece, lat_steps, still)
    corner = moved(by_segment(columns(row_piece), lon_steps), lat_steps, lon_steps)
    beside = moved(by_segment(columns(field), lon_steps), still, lon_steps)
    block_count, row_count, column_count, width = field.shape

    def joined(own, other, axis, start, half, size):
        def make(step):
            pair = [own, other] if step > 0 else [other, own]
            return lax.dynamic_slice_in_dim(
                jnp.concatenate(pair, axis=axis), start if step > 0 else half + start, size, axis
            )

        return make

    near = by_segment(joined(field, beside, 2, lon_shift, HALF_LON, column_count), lon_steps)
    far = by_segment(joined(below, corner, 2, lon_shift, HALF_LON, column_count), lon_steps)
    return by_segment(joined(near, far, 1, lat_shift, HALF_LAT, row_count), lat_steps)


def shift(field, lat_shift, lon_shift):
    choice = 2 * (lat_shift < 0).astype(jnp.int32) + (lon_shift < 0).astype(jnp.int32)
    ways = [functools.partial(shift_one_way, (a, a), (b, b)) for a in (1, -1) for b in (1, -1)]
    return lax.switch(choice, ways, field, lat_shift, lon_shift)


def shift_each(field, lat_shifts, lon_shifts):
    other = jnp.where((lat_shifts[1] < 0) | (lon_shifts[1] < 0), 1, 0)
    lat_other, lon_other = lat_shifts[other], lon_shifts[other]
    choice = 4 * other + 2 * (lat_other < 0).astype(jnp.int32) + (lon_other < 0).astype(jnp.int32)
    ways = []
    for segment in (0, 1):
        for a in (1, -1):
            for b in (1, -1):
                lat_steps = (a, 1) if segment == 0 else (1, a)
                lon_steps = (b, 1) if segment == 0 else (1, b)
                ways.append(functools.partial(shift_one_way, lat_steps, lon_steps))
    own = lax.axis_index("segment")
    return lax.switch(choice, ways, field, lat_shifts[own], lon_shifts[own])


def body(latents, land_mask, land_embed, qkv_weight, out_weight, norm_gain, offsets):
    segment_index = lax.axis_index("segment")
    block_count, row_count, column_count, width = latents.shape
    assert (row_count, column_count) == (WLAT, WLON)
    total_rows = row_count * lax.axis_size("lat")
    land_term = land_mask.astype(jnp.float32)[None, :, :, None] * land_embed.astype(jnp.float32)
    seeded = (latents.astype(jnp.float32) + land_term).astype(jnp.bfloat16)
    wqkv = qkv_weight[0]
    wout = out_weight[0]
    gain = lax.dynamic_index_in_dim(norm_gain, segment_index, 0, False)
    lat_offset, lon_offset = offsets[:, 0], offsets[:, 1]
    lat_base = jnp.where(lat_offset >= HALF_LAT, lat_offset - WLAT, lat_offset)
    lon_base = jnp.where(lon_offset >= HALF_LON, lon_offset - WLON, lon_offset)

    def codes_of(s):
        held = lax.axis_index("lat") * row_count + jnp.arange(row_count, dtype=jnp.int32) + lat_base[s]
        wrapped = (held % total_rows < lat_offset[s]).astype(jnp.int32)
        blocks = 2 * jnp.arange(block_count, dtype=jnp.int32)
        codes = jnp.broadcast_to(
            blocks[:, None, None] + wrapped[None, :, None], (block_count, row_count, column_count)
        )
        return codes.reshape(-1)

    first_in = shift(seeded, lat_base[0], lon_base[0])
    first = attend(first_in, codes_of(0), wqkv, wout, gain)
    passed = lax.ppermute(first, "segment", [(0, 1)])
    second_in = shift(passed, lat_base[1] - lat_base[0], lon_base[1] - lon_base[0])
    second = attend(second_in, codes_of(1), wqkv, wout, gain)
    merged = jnp.where(segment_index == 0, first, second)
    return shift_each(merged, -lat_base, -lon_base)[None]


def solution(mesh):
    return jax.shard_map(
        body,
        mesh=mesh,
        in_specs=(
            P(None, "lat", "lon", None),
            P("lat", "lon"),
            P(),
            P("segment", None, None),
            P("segment", None, None),
            P(),
            P(),
        ),
        out_specs=P("segment", None, "lat", "lon", None),
        check_vma=False,
    )
```

time: 142 us -> 84.5 us (0.60)
  waiting for transfers between devices: 70.5 us -> 13.1 us
  matrix products: 23.3 us -> 0 us
  Pallas kernels: 0 us -> 15 us
  loops' own time: 0 us -> 9.22 us
  local copies, waits for them, and re-layouts: 24.4 us -> 16.6 us
  starting transfers between devices: 8.58 us -> 13.4 us
  other arithmetic: 7.6 us -> 9.45 us
    ppermute x9 -> x10, waiting for transfers between devices: 70.5 us -> 13.1 us  [the longest x9 9.44 us: moved(): return lax.ppermute(piece, ('segment', 'lon', 'lat'), route)]
    dot_general x8 -> x0, matrix products: 19.8 us -> none  [the longest x2 7.76 us: attend(): jnp.dot(flat, wqkv, preferred_element_type=jnp.float32).astype(jnp.bfloat16)]
    pallas_call x0 -> x2, Pallas kernels: none -> 15 us  [attend(): pl.pallas_call(functools.partial(attend_kernel, head_size=head_size), gri...]
    another operation x0 -> x3, loops' own time: none -> 9.22 us  [the longest x1 4.87 us: shift_each(): return lax.switch(choice, ways, field, lat_shifts[own], lon_shifts[own])]
    ppermute x9 -> x10, starting transfers between devices: 8.58 us -> 13.4 us  [the longest x9 12.2 us: moved(): return lax.ppermute(piece, ('segment', 'lon', 'lat'), route)]
    reshape x4, local copies, waits for them, and re-layouts: 4.91 us -> 0.27 us  [the longest x2 0.14 us: attend(): flat = field.reshape(-1, width)]
    sub x2 -> x0, matrix products: 3.46 us -> none  [attend(): probs = jax.nn.softmax(scores, axis=-1).astype(jnp.bfloat16)]
    convert_element_type x2 -> x0, local copies, waits for them, and re-layouts: 3.03 us -> none  [attend(): attended = attended.astype(jnp.bfloat16).reshape(-1, width)]
  transfers between devices with their start and end apart: 9 -> 10, of which waited for: 8 -> 4; matrix products, arithmetic and copies ran while one was open for 1% -> 7% of each run, Pallas kernels for 0% -> 0%
where the time goes in v1:
time: 84.5 us; the launch traced here: 83.4 us
  local copies, waits for them, and re-layouts  16.6 us (20%)
  Pallas kernels  15 us (18%)
  starting transfers between devices  13.4 us (16%)
  waiting for transfers between devices  13.1 us (16%)
  other arithmetic  9.45 us (11%)
  loops' own time  9.22 us (11%)
  between operations  6.59 us (8%)
    pallas_call x2, Pallas kernels, attend(): pl.pallas_call(functools.partial(attend_kernel, head_size=head_size), gri...  15 us
    ppermute x9, starting transfers between devices, moved(): return lax.ppermute(piece, ('segment', 'lon', 'lat'), route)  12.2 us
    ppermute x9, waiting for transfers between devices, moved(): return lax.ppermute(piece, ('segment', 'lon', 'lat'), route)  9.44 us
    unnamed x12, local copies, waits for them, and re-layouts  6.99 us
    another operation x1, loops' own time, shift_each(): return lax.switch(choice, ways, field, lat_shifts[own], lon_shifts[own])  4.87 us
    another operation x2, loops' own time, shift(): return lax.switch(choice, ways, field, lat_shift, lon_shift)  4.34 us
    ppermute x1, waiting for transfers between devices, body(): passed = lax.ppermute(first, 'segment', [(0, 1)])  3.62 us
    concatenate x6, other arithmetic, make(): jnp.concatenate(pair, axis=axis)  2.98 us
  transfers between devices with their start and end apart: 10, of which 4 were waited for; matrix products, arithmetic and copies ran while one was open for 7% of the time, Pallas kernels for 0%

profile of v1, /device:TPU:4, one launch (start us, length us, event | category | flops | bytes accessed | tf_op | source)
XLA Modules:
  0.0 83.4 jit_solution(12902485313148208307)
XLA Ops:
  0.0 1.0 %slice_reduce_fusion = (s32[2]{0:T(128)S(1)}, s32[2]{0:T(128)S(1)}) fusion(s32[2,2]{1,0:T(2,128)} %param.29), kind=kLoop, calls=%fused_computation.228 | loop fusion | bytes 32 | tf_op jit(solution)/shard_map/slice | solution.py:168
  1.0 1.3 %fusion.82 = (s32[1,1]{1,0:T(1,128)}, s32[1,1]{1,0:T(1,128)}) fusion(s32[2,2]{1,0:T(2,128)} %param.29), kind=kLoop, calls=%fused_computation.237 | loop fusion | bytes 16 | tf_op jit(solution)/shard_map/slice | solution.py:174
  2.3 0.6 fusion.84
  2.9 1.3 %compare_convert_fusion = s32[6]{0:T(128)S(1)} fusion(s32[]{:T(128)} %bitcast.32, s32[]{:T(128)} %bitcast.29, s32[]{:T(128)S(6)} %mul.46), kind=kLoop, calls=%fused_computation.224 | loop fusion | flops 60 | bytes 36 | tf_op jit(solution)/shard_map/convert_element_type | solution.py:174
  4.2 1.2 %compare_convert_fusion.1 = s32[6]{0:T(128)S(1)} fusion(s32[]{:T(128)} %bitcast.28, s32[]{:T(128)} %bitcast.27, s32[]{:T(128)S(6)} %mul.46), kind=kLoop, calls=%fused_computation.226 | loop fusion | flops 60 | bytes 36 | tf_op jit(solution)/shard_map/convert_element_type | solution.py:174
  5.8 0.6 fusion.83
  6.4 0.7 convert_element_type.48
  7.0 0.7 convert_element_type.49
  9.2 1.0 %add_convert_fusion = bf16[2,6,12,1024]{3,2,1,0:T(8,128)(2,1)S(1)} fusion(bf16[2,6,12,1024]{3,0,2,1:T(2,128)(2,1)} %param.23, f32[6,12,1024]{2,1,0:T(8,128)S(1)} %broadcast_multiply_fusion), kind=kLoop, calls=%fused_computation.220 | loop fusion | flops 442368 | bytes 884736 | tf_op jit(solution)/shard_map/convert_element_type | solution.py:164
  10.3 12.0 %conditional.3 = (bf16[144,1024]{1,0:T(8,128)(2,1)S(1)}) conditional(s32[]{:T(128)} %clamp.11, (bf16[2,6,12,1024]{3,2,1,0:T(8,128)(2,1)S(1)}, s32[]{:T(128)}, s32[]{:T(128)}) %tuple.69, (bf16[2,6,12,1024]{3,2,1,0:T(8,128)(2,1)S(1)}, s32[]{:T(128)}, s32[]{:T(128)}) %tuple.69, (bf16[2,6,12,1024]{3,2,1,0:T(8,128)(2,1)S(1)}, ...), branch_computations={%region_0.1_spmd, %region_1.2_spmd, %region_2.3_spmd, %region_3.4_... | conditional | flops 1032200 | bytes 4645096 | solution.py:140
  10.3 1.0 %collective-permute-start = (bf16[2,6,6,1024]{3,2,1,0:T(8,128)(2,1)S(1)}, bf16[2,6,6,1024]{3,2,1,0:T(8,128)(2,1)S(1)}, u32[]{:S(2)}, u32[]{:S(2)}) collective-permute-start(bf16[2,6,6,1024]{3,2,1,0:T(8,128)(2,1)S(1)} %slice.162), channel_id=1, source_target_pairs={{4,0},{5,1},{6,2},{7,3},{8,4},{9,5},{10,6},{11,7},{12,8},{13,9},{1... | collective-permute-start | bytes 442376 | tf_op jit(solution)/shard_map/cond/branch_0_fun/ppermute | solution.py:104
  11.3 3.7 %collective-permute-start.1 = (bf16[2,3,12,1024]{3,2,1,0:T(8,128)(2,1)S(1)}, bf16[2,3,12,1024]{3,2,1,0:T(8,128)(2,1)S(1)}, u32[]{:S(2)}, u32[]{:S(2)}) collective-permute-start(bf16[2,3,12,1024]{3,2,1,0:T(8,128)(2,1)S(1)} %slice.163), channel_id=1, source_target_pairs={{1,0},{2,1},{3,2},{0,3},{5,4},{6,5},{7,6},{4,7},{9,8},{10,9},{11,1... | collective-permute-start | bytes 442376 | tf_op jit(solution)/shard_map/cond/branch_0_fun/ppermute | solution.py:104
  15.0 0.3 collective-permute-start.2
  19.4 0.3 fusion.1
  19.7 1.2 %collective-permute-done.2 = bf16[2,3,6,1024]{3,2,1,0:T(8,128)(2,1)} collective-permute-done((bf16[2,3,6,1024]{3,2,1,0:T(8,128)(2,1)S(1)}, bf16[2,3,6,1024]{3,2,1,0:T(8,128)(2,1)}, u32[]{:S(2)}, u32[]{:S(2)}) %collective-permute-start.2) | collective-permute-done | bytes 73760 | tf_op jit(solution)/shard_map/cond/branch_0_fun/ppermute | solution.py:104
  21.0 1.1 %fusion.2 = bf16[2,3,12,1024]{3,2,1,0:T(8,128)(2,1)S(1)} fusion(s32[]{:T(128)S(6)} %select_n.268, bf16[2,3,12,1024]{3,2,1,0:T(8,128)(2,1)S(1)} %collective-permute-done.1, bf16[2,3,6,1024]{3,2,1,0:T(8,128)(2,1)} %collective-permute-done.2), kind=kLoop, calls=%fused_computation.8 | loop fusion | flops 294912 | bytes 368644 | tf_op jit(solution)/shard_map/cond/branch_0_fun/concatenate | solution.py:127
  22.0 0.2 fusion
  22.4 2.8 %copy-done.1 = bf16[1,1024,3072]{2,1,0:T(8,128)(2,1)S(1)} copy-done((bf16[1,1024,3072]{2,1,0:T(8,128)(2,1)S(1)}, bf16[1,1024,3072]{2,1,0:T(8,128)(2,1)}, u32[]{:S(2)}) %copy-start.1) | copy-done | bytes 6291480
  25.1 7.1 %shard_map.81 = bf16[144,1024]{1,0:T(8,128)(2,1)S(1)} custom-call(s32[144,1]{1,0:T(8,128)S(1)} %broadcast_in_dim_reshape.17.col_code, s32[1,144]{1,0:T(1,128)S(1)} %broadcast_in_dim_reshape.15.row_code, bf16[144,1024]{1,0:T(8,128)(2,1)S(1)} %get-tuple-element.349.x_ref, bf16[1024,3072]{1,0:T(8,128)(2,1)S(1)} %bitcast.43, bf16[1024,3072]{1,0:T(8,128)(2,1)S(1)} %bitcast.44, ...), custom_call_target="tpu_custom_call" | custom-call | flops 1207959552 | bytes 8388608 | tf_op jit(solution)/shard_map/pallas_call | solution.py:71
  32.4 1.3 %collective-permute-start.48 = (bf16[2,6,12,1024]{3,2,1,0:T(8,128)(2,1)S(1)}, bf16[2,6,12,1024]{3,2,1,0:T(8,128)(2,1)S(1)}, u32[]{:S(2)}, u32[]{:S(2)}) collective-permute-start(bf16[2,6,12,1024]{3,2,1,0:T(8,128)(2,1)S(1)} %reshape.165), channel_id=1, source_target_pairs={{0,16},{1,17},{2,18},{3,19},{4,20},{5,21},{6,22},{7,23},{8,24},{9,... | collective-permute-start | bytes 884744 | tf_op jit(solution)/shard_map/ppermute | solution.py:183
  35.2 0.6 slice.233
  35.8 0.6 slice.235
  37.6 0.6 dynamic_slice.240
  38.2 0.7 dynamic_slice.241
  41.4 3.6 %collective-permute-done.48 = bf16[2,6,12,1024]{3,2,1,0:T(8,128)(2,1)S(1)} collective-permute-done((bf16[2,6,12,1024]{3,2,1,0:T(8,128)(2,1)S(1)}, bf16[2,6,12,1024]{3,2,1,0:T(8,128)(2,1)S(1)}, u32[]{:S(2)}, u32[]{:S(2)}) %collective-permute-start.48) | collective-permute-done | bytes 294944 | tf_op jit(solution)/shard_map/ppermute | solution.py:183
  45.0 14.5 %conditional.4 = (bf16[144,1024]{1,0:T(8,128)(2,1)S(1)}) conditional(s32[]{:T(128)} %clamp.10, (bf16[2,6,12,1024]{3,2,1,0:T(8,128)(2,1)S(1)}, s32[]{:T(128)}, s32[]{:T(128)}) %tuple.70, (bf16[2,6,12,1024]{3,2,1,0:T(8,128)(2,1)S(1)}, s32[]{:T(128)}, s32[]{:T(128)}) %tuple.70, (bf16[2,6,12,1024]{3,2,1,0:T(8,128)(2,1)S(1)}, ...), branch_computations={%region_4.5_spmd, %region_5.6_spmd, %region_6.7_spmd, %region_7.8_... | conditional | flops 1032200 | bytes 4645096 | solution.py:140
  45.0 0.7 slice.185
  45.7 0.7 slice.184
  46.4 1.7 %collective-permute-start.22 = (bf16[2,3,12,1024]{3,2,1,0:T(8,128)(2,1)}, bf16[2,3,12,1024]{3,2,1,0:T(8,128)(2,1)S(1)}, u32[]{:S(2)}, u32[]{:S(2)}) collective-permute-start(bf16[2,3,12,1024]{3,2,1,0:T(8,128)(2,1)} %slice.184), channel_id=1, source_target_pairs={{3,0},{0,1},{1,2},{2,3},{7,4},{4,5},{5,6},{6,7},{11,8},{8,9},{9,10... | collective-permute-start | bytes 442376 | tf_op jit(solution)/shard_map/cond/branch_3_fun/ppermute | solution.py:104
  48.1 1.5 %collective-permute-start.21 = (bf16[2,3,6,1024]{3,2,1,0:T(8,128)(2,1)S(1)}, bf16[2,3,6,1024]{3,2,1,0:T(8,128)(2,1)}, u32[]{:S(2)}, u32[]{:S(2)}) collective-permute-start(bf16[2,3,6,1024]{3,2,1,0:T(8,128)(2,1)S(1)} %slice.183), channel_id=1, source_target_pairs={{15,0},{12,1},{13,2},{14,3},{3,4},{0,5},{1,6},{2,7},{7,8},{4,9},{5... | collective-permute-start | bytes 221192 | tf_op jit(solution)/shard_map/cond/branch_3_fun/ppermute | solution.py:104
  49.6 1.4 %collective-permute-done.23 = bf16[2,6,6,1024]{3,2,1,0:T(8,128)(2,1)S(1)} collective-permute-done((bf16[2,6,6,1024]{3,2,1,0:T(8,128)(2,1)}, bf16[2,6,6,1024]{3,2,1,0:T(8,128)(2,1)S(1)}, u32[]{:S(2)}, u32[]{:S(2)}) %collective-permute-start.23) | collective-permute-done | bytes 147488 | tf_op jit(solution)/shard_map/cond/branch_3_fun/ppermute | solution.py:104
  51.0 0.3 fusion.22
  51.3 6.8 %collective-permute-done.21 = bf16[2,3,6,1024]{3,2,1,0:T(8,128)(2,1)} collective-permute-done((bf16[2,3,6,1024]{3,2,1,0:T(8,128)(2,1)S(1)}, bf16[2,3,6,1024]{3,2,1,0:T(8,128)(2,1)}, u32[]{:S(2)}, u32[]{:S(2)}) %collective-permute-start.21) | collective-permute-done | bytes 73760 | tf_op jit(solution)/shard_map/cond/branch_3_fun/ppermute | solution.py:104
  58.1 1.0 %fusion.23 = bf16[2,3,12,1024]{3,2,1,0:T(8,128)(2,1)S(1)} fusion(s32[]{:T(128)S(6)} %select_n.282, bf16[2,3,6,1024]{3,2,1,0:T(8,128)(2,1)} %collective-permute-done.21, bf16[2,3,12,1024]{3,2,1,0:T(8,128)(2,1)S(1)} %collective-permute-done.22), kind=kLoop, calls=%fused_computation.71 | loop fusion | flops 294912 | bytes 368644 | tf_op jit(solution)/shard_map/cond/branch_3_fun/concatenate | solution.py:127
  59.5 0.7 copy-done.4
  60.2 2.8 %copy-done.2 = bf16[1,1024,3072]{2,1,0:T(8,128)(2,1)S(1)} copy-done((bf16[1,1024,3072]{2,1,0:T(8,128)(2,1)S(1)}, bf16[1,1024,3072]{2,1,0:T(8,128)(2,1)}, u32[]{:S(2)}) %copy-start.2) | copy-done | bytes 6291480
  63.0 7.8 %shard_map.82 = bf16[144,1024]{1,0:T(8,128)(2,1)S(1)} custom-call(s32[144,1]{1,0:T(8,128)S(1)} %broadcast_in_dim_reshape.16.col_code, s32[1,144]{1,0:T(1,128)S(1)} %broadcast_in_dim_reshape.13.row_code, bf16[144,1024]{1,0:T(8,128)(2,1)} %copy-done.4, bf16[1024,3072]{1,0:T(8,128)(2,1)S(1)} %bitcast.46, bf16[1024,3072]{1,0:T(8,128)(2,1)S(1)} %bitcast.47, ...), custom_call_target="tpu_custom_call" | custom-call | flops 1207959552 | bytes 8388608 | tf_op jit(solution)/shard_map/pallas_call | solution.py:71
  70.8 11.8 %conditional.5 = (bf16[1,2,6,12,1024]{4,1,3,2,0:T(2,128)(2,1)S(1)}) conditional(s32[]{:T(128)} %clamp.9, (s32[]{:T(128)}, bf16[144,1024]{1,0:T(8,128)(2,1)S(1)}, bf16[2,6,12,1024]{3,2,1,0:T(8,128)(2,1)S(1)}, s32[2]{0:T(128)S(1)}, s32[]{:T(128)}, /*index=5*/s32[2]{0:T(128)S(1)}) %tuple.71, (s32[]{:T(128)}, ...), branch_computations={%region_8.9_spmd, %region_9.10_spmd, %region_10.11_spmd, %region_1... | conditional | flops 2764819 | bytes 6488457 | solution.py:155
  71.0 1.5 %collective-permute-start.29 = (bf16[2,3,12,1024]{3,2,1,0:T(8,128)(2,1)S(1)}, bf16[2,3,12,1024]{3,2,1,0:T(8,128)(2,1)S(1)}, u32[]{:S(2)}, u32[]{:S(2)}) collective-permute-start(bf16[2,3,12,1024]{3,2,1,0:T(8,128)(2,1)S(1)} %slice.249), channel_id=1, source_target_pairs={{1,0},{2,1},{3,2},{0,3},{5,4},{6,5},{7,6},{4,7},{9,8},{10,9},{11,1... | collective-permute-start | bytes 442376 | tf_op jit(solution)/shard_map/cond/branch_1_fun/ppermute | solution.py:104
  72.6 1.3 %collective-permute-start.27 = (bf16[2,6,6,1024]{3,2,1,0:T(8,128)(2,1)S(1)}, bf16[2,6,6,1024]{3,2,1,0:T(8,128)(2,1)S(1)}, u32[]{:S(2)}, u32[]{:S(2)}) collective-permute-start(bf16[2,6,6,1024]{3,2,1,0:T(8,128)(2,1)S(1)} %slice_select_fusion), channel_id=1, source_target_pairs={{12,0},{13,1},{14,2},{15,3},{0,4},{1,5},{2,6},{3,7},{4,8},{5,9},{6... | collective-permute-start | bytes 442376 | tf_op jit(solution)/shard_map/cond/branch_1_fun/ppermute | solution.py:104
  73.9 1.2 %collective-permute-start.28 = (bf16[2,3,6,1024]{3,2,1,0:T(8,128)(2,1)S(1)}, bf16[2,3,6,1024]{3,2,1,0:T(8,128)(2,1)S(1)}, u32[]{:S(2)}, u32[]{:S(2)}) collective-permute-start(bf16[2,3,6,1024]{3,2,1,0:T(8,128)(2,1)S(1)} %slice_select_fusion.1), channel_id=1, source_target_pairs={{13,0},{14,1},{15,2},{12,3},{1,4},{2,5},{3,6},{0,7},{5,8},{6,9},{7... | collective-permute-start | bytes 221192 | tf_op jit(solution)/shard_map/cond/branch_1_fun/ppermute | solution.py:104
  75.1 0.6 dynamic_slice.190
  78.0 0.6 dynamic_slice.195
  81.1 0.7 fusion.31
  81.8 0.4 fusion.34
  82.1 0.2 fusion.29
  82.3 0.3 copy.23
  82.7 0.7 copy-done.5
  (39 shorter events, 1.3 us)
Async XLA Ops:
  0.0 22.3 %copy-start = (f32[2,1024]{1,0:T(2,128)S(1)}, f32[2,1024]{1,0:T(2,128)}, u32[]{:S(2)}) copy-start(f32[2,1024]{1,0:T(2,128)} %param.28) | copy-start | bytes 24580
  10.3 12.1 %copy-start.3 = (bf16[1,1024,1024]{2,1,0:T(8,128)(2,1)S(1)}, bf16[1,1024,1024]{2,1,0:T(8,128)(2,1)}, u32[]{:S(2)}) copy-start(bf16[1,1024,1024]{2,1,0:T(8,128)(2,1)} %param.27) | copy-start | bytes 6291460
  10.3 9.1 %collective-permute-start = (bf16[2,6,6,1024]{3,2,1,0:T(8,128)(2,1)S(1)}, bf16[2,6,6,1024]{3,2,1,0:T(8,128)(2,1)S(1)}, u32[]{:S(2)}, u32[]{:S(2)}) collective-permute-start(bf16[2,6,6,1024]{3,2,1,0:T(8,128)(2,1)S(1)} %slice.162), channel_id=1, source_target_pairs={{4,0},{5,1},{6,2},{7,3},{8,4},{9,5},{10,6},{11,7},{12,8},{13,9},{1... | collective-permute-start | bytes 442376 | tf_op jit(solution)/shard_map/cond/branch_0_fun/ppermute | solution.py:104
  11.3 9.7 %collective-permute-start.1 = (bf16[2,3,12,1024]{3,2,1,0:T(8,128)(2,1)S(1)}, bf16[2,3,12,1024]{3,2,1,0:T(8,128)(2,1)S(1)}, u32[]{:S(2)}, u32[]{:S(2)}) collective-permute-start(bf16[2,3,12,1024]{3,2,1,0:T(8,128)(2,1)S(1)} %slice.163), channel_id=1, source_target_pairs={{1,0},{2,1},{3,2},{0,3},{5,4},{6,5},{7,6},{4,7},{9,8},{10,9},{11,1... | collective-permute-start | bytes 442376 | tf_op jit(solution)/shard_map/cond/branch_0_fun/ppermute | solution.py:104
  15.0 6.0 %collective-permute-start.2 = (bf16[2,3,6,1024]{3,2,1,0:T(8,128)(2,1)S(1)}, bf16[2,3,6,1024]{3,2,1,0:T(8,128)(2,1)}, u32[]{:S(2)}, u32[]{:S(2)}) collective-permute-start(bf16[2,3,6,1024]{3,2,1,0:T(8,128)(2,1)S(1)} %slice.164), channel_id=1, source_target_pairs={{5,0},{6,1},{7,2},{4,3},{9,4},{10,5},{11,6},{8,7},{13,8},{14,9},{1... | collective-permute-start | bytes 221192 | tf_op jit(solution)/shard_map/cond/branch_0_fun/ppermute | solution.py:104
  22.3 2.8 %copy-start.1 = (bf16[1,1024,3072]{2,1,0:T(8,128)(2,1)S(1)}, bf16[1,1024,3072]{2,1,0:T(8,128)(2,1)}, u32[]{:S(2)}) copy-start(bf16[1,1024,3072]{2,1,0:T(8,128)(2,1)} %param.26) | copy-start | bytes 18874372
  32.4 12.6 %collective-permute-start.48 = (bf16[2,6,12,1024]{3,2,1,0:T(8,128)(2,1)S(1)}, bf16[2,6,12,1024]{3,2,1,0:T(8,128)(2,1)S(1)}, u32[]{:S(2)}, u32[]{:S(2)}) collective-permute-start(bf16[2,6,12,1024]{3,2,1,0:T(8,128)(2,1)S(1)} %reshape.165), channel_id=1, source_target_pairs={{0,16},{1,17},{2,18},{3,19},{4,20},{5,21},{6,22},{7,23},{8,24},{9,... | collective-permute-start | bytes 884744 | tf_op jit(solution)/shard_map/ppermute | solution.py:183
  45.7 5.3 %collective-permute-start.23 = (bf16[2,6,6,1024]{3,2,1,0:T(8,128)(2,1)}, bf16[2,6,6,1024]{3,2,1,0:T(8,128)(2,1)S(1)}, u32[]{:S(2)}, u32[]{:S(2)}) collective-permute-start(bf16[2,6,6,1024]{3,2,1,0:T(8,128)(2,1)} %slice.185), channel_id=1, source_target_pairs={{12,0},{13,1},{14,2},{15,3},{0,4},{1,5},{2,6},{3,7},{4,8},{5,9},{6... | collective-permute-start | bytes 442376 | tf_op jit(solution)/shard_map/cond/branch_3_fun/ppermute | solution.py:104
  46.4 11.7 %collective-permute-start.22 = (bf16[2,3,12,1024]{3,2,1,0:T(8,128)(2,1)}, bf16[2,3,12,1024]{3,2,1,0:T(8,128)(2,1)S(1)}, u32[]{:S(2)}, u32[]{:S(2)}) collective-permute-start(bf16[2,3,12,1024]{3,2,1,0:T(8,128)(2,1)} %slice.184), channel_id=1, source_target_pairs={{3,0},{0,1},{1,2},{2,3},{7,4},{4,5},{5,6},{6,7},{11,8},{8,9},{9,10... | collective-permute-start | bytes 442376 | tf_op jit(solution)/shard_map/cond/branch_3_fun/ppermute | solution.py:104
  48.1 10.0 %collective-permute-start.21 = (bf16[2,3,6,1024]{3,2,1,0:T(8,128)(2,1)S(1)}, bf16[2,3,6,1024]{3,2,1,0:T(8,128)(2,1)}, u32[]{:S(2)}, u32[]{:S(2)}) collective-permute-start(bf16[2,3,6,1024]{3,2,1,0:T(8,128)(2,1)S(1)} %slice.183), channel_id=1, source_target_pairs={{15,0},{12,1},{13,2},{14,3},{3,4},{0,5},{1,6},{2,7},{7,8},{4,9},{5... | collective-permute-start | bytes 221192 | tf_op jit(solution)/shard_map/cond/branch_3_fun/ppermute | solution.py:104
  59.5 0.7 copy-start.4
  60.2 2.8 %copy-start.2 = (bf16[1,1024,3072]{2,1,0:T(8,128)(2,1)S(1)}, bf16[1,1024,3072]{2,1,0:T(8,128)(2,1)}, u32[]{:S(2)}) copy-start(bf16[1,1024,3072]{2,1,0:T(8,128)(2,1)} %param.26) | copy-start | bytes 18874372
  71.0 10.7 %collective-permute-start.29 = (bf16[2,3,12,1024]{3,2,1,0:T(8,128)(2,1)S(1)}, bf16[2,3,12,1024]{3,2,1,0:T(8,128)(2,1)S(1)}, u32[]{:S(2)}, u32[]{:S(2)}) collective-permute-start(bf16[2,3,12,1024]{3,2,1,0:T(8,128)(2,1)S(1)} %slice.249), channel_id=1, source_target_pairs={{1,0},{2,1},{3,2},{0,3},{5,4},{6,5},{7,6},{4,7},{9,8},{10,9},{11,1... | collective-permute-start | bytes 442376 | tf_op jit(solution)/shard_map/cond/branch_1_fun/ppermute | solution.py:104
  72.6 8.5 %collective-permute-start.27 = (bf16[2,6,6,1024]{3,2,1,0:T(8,128)(2,1)S(1)}, bf16[2,6,6,1024]{3,2,1,0:T(8,128)(2,1)S(1)}, u32[]{:S(2)}, u32[]{:S(2)}) collective-permute-start(bf16[2,6,6,1024]{3,2,1,0:T(8,128)(2,1)S(1)} %slice_select_fusion), channel_id=1, source_target_pairs={{12,0},{13,1},{14,2},{15,3},{0,4},{1,5},{2,6},{3,7},{4,8},{5,9},{6... | collective-permute-start | bytes 442376 | tf_op jit(solution)/shard_map/cond/branch_1_fun/ppermute | solution.py:104
  73.9 7.9 %collective-permute-start.28 = (bf16[2,3,6,1024]{3,2,1,0:T(8,128)(2,1)S(1)}, bf16[2,3,6,1024]{3,2,1,0:T(8,128)(2,1)S(1)}, u32[]{:S(2)}, u32[]{:S(2)}) collective-permute-start(bf16[2,3,6,1024]{3,2,1,0:T(8,128)(2,1)S(1)} %slice_select_fusion.1), channel_id=1, source_target_pairs={{13,0},{14,1},{15,2},{12,3},{1,4},{2,5},{3,6},{0,7},{5,8},{6,9},{7... | collective-permute-start | bytes 221192 | tf_op jit(solution)/shard_map/cond/branch_1_fun/ppermute | solution.py:104
  82.6 0.7 copy-start.5

commit v2 on v1

--- a/solution.py
+++ b/solution.py
@@ -18,13 +18,30 @@
 NT = (((1,), (1,)), ((), ()))
 
 
-def attend_kernel(col_code, row_code, x_ref, wq_ref, wk_ref, wv_ref, wo_ref, gain_ref, out_ref, total, *, head_size):
+def cell_codes(place_ref, shape, axis, total_rows):
+    cell = lax.broadcasted_iota(jnp.int32, shape, axis)
+    line = jnp.zeros(shape, jnp.int32)
+    for start in range(WLON, shape[axis], WLON):
+        line += (cell >= start).astype(jnp.int32)
+    block = jnp.zeros(shape, jnp.int32)
+    for start in range(WLAT, shape[axis] // WLON, WLAT):
+        block += (line >= start).astype(jnp.int32)
+    held = place_ref[0] + line - WLAT * block
+    held = jnp.where(held < 0, held + total_rows, held)
+    held = jnp.where(held >= total_rows, held - total_rows, held)
+    return 2 * block + (held < place_ref[1]).astype(jnp.int32)
+
+
+def attend_kernel(place_ref, x_ref, wq_ref, wk_ref, wv_ref, wo_ref, gain_ref, out_ref, total, *, head_size, total_rows):
     step = pl.program_id(0)
     x = x_ref[...]
     q = jnp.dot(x, wq_ref[...], preferred_element_type=jnp.float32).astype(jnp.bfloat16)
     k = jnp.dot(x, wk_ref[...], preferred_element_type=jnp.float32).astype(jnp.bfloat16)
     v = jnp.dot(x, wv_ref[...], preferred_element_type=jnp.float32).astype(jnp.bfloat16)
-    allowed = col_code[...] == row_code[...]
+    cells = x.shape[0]
+    allowed = (
+        cell_codes(place_ref, (cells, 1), 0, total_rows) == cell_codes(place_ref, (1, cells), 1, total_rows)
+    )
     scale = 1.0 / math.sqrt(head_size)
     first_half = lax.broadcasted_iota(jnp.int32, (x.shape[0], PAIR), 1) < head_size
     parts = []
@@ -61,7 +78,7 @@
         out_ref[...] = (x.astype(jnp.float32) + branch).astype(jnp.bfloat16)
 
 
-def attend(field, codes, wqkv, wout, gain):
+def attend(field, place, wqkv, wout, gain):
     width = field.shape[-1]
     flat = field.reshape(-1, width)
     cells = flat.shape[0]
@@ -69,12 +86,13 @@
     head_size = width // HEADS
     full = lambda shape: pl.BlockSpec(shape, lambda p: (0, 0))
     out = pl.pallas_call(
-        functools.partial(attend_kernel, head_size=head_size),
+        functools.partial(
+            attend_kernel, head_size=head_size, total_rows=WLAT * lax.axis_size("lat")
+        ),
         grid=(STEPS,),
         out_shape=jax.ShapeDtypeStruct((cells, width), jnp.bfloat16),
         in_specs=[
-            full((cells, 1)),
-            full((1, cells)),
+            pl.BlockSpec(memory_space=pltpu.SMEM),
             full((cells, width)),
             pl.BlockSpec((width, slab), lambda p: (0, p)),
             pl.BlockSpec((width, slab), lambda p: (0, p + STEPS)),
@@ -84,24 +102,64 @@
         ],
         out_specs=full((cells, width)),
         scratch_shapes=[pltpu.VMEM((cells, width), jnp.float32)],
-        compiler_params=pltpu.CompilerParams(vmem_limit_bytes=24 * 1024 * 1024),
+        compiler_params=pltpu.CompilerParams(vmem_limit_bytes=56 * 1024 * 1024),
         cost_estimate=pl.CostEstimate(
             flops=8 * cells * width * width, bytes_accessed=8 * width * width, transcendentals=HEADS * cells * cells
         ),
-    )(codes[:, None], codes[None, :], flat, wqkv, wqkv, wqkv, wout, gain[None, :])
+    )(place, flat, wqkv, wqkv, wqkv, wout, gain[None, :])
     return out.reshape(field.shape)
 
 
-def moved(piece, lat_steps, lon_steps):
-    segments, lons, lats = (lax.axis_size(axis) for axis in ("segment", "lon", "lat"))
-    place = lambda s, j, i: (s * lons + j % lons) * lats + i % lats
-    route = [
-        (place(s, j + lon_steps[s], i + lat_steps[s]), place(s, j, i))
-        for s in range(segments)
-        for j in range(lons)
-        for i in range(lats)
-    ]
-    return lax.ppermute(piece, ("segment", "lon", "lat"), route)
+def exchange_kernel(lat_steps, lon_steps, below_in, corner_in, beside_in, below, corner, beside, send_sem, recv_sem):
+    segment, lon, lat = (lax.axis_index(axis) for axis in ("segment", "lon", "lat"))
+    lons, lats = lax.axis_size("lon"), lax.axis_size("lat")
+    pick = lambda steps: steps[0] + segment * (steps[1] - steps[0])
+    lat_step, lon_step = pick(lat_steps), pick(lon_steps)
+    place = lambda a, b: (segment, lax.rem(lon + b + lons, lons), lax.rem(lat + a + lats, lats))
+    ways = ((lat_step, lon_step), (lat_step, 0), (0, lon_step))
+    barrier = pltpu.get_barrier_semaphore()
+    for a, b in ways:
+        pl.semaphore_signal(barrier, inc=1, device_id=place(a, b), device_id_type=pl.DeviceIdType.MESH)
+    pl.semaphore_wait(barrier, 3)
+    copies = []
+    for index, ((a, b), source, target) in enumerate(
+        zip(ways, (corner_in, below_in, beside_in), (corner, below, beside))
+    ):
+        copy = pltpu.make_async_remote_copy(
+            src_ref=source,
+            dst_ref=target,
+            send_sem=send_sem.at[index],
+            recv_sem=recv_sem.at[index],
+            device_id=place(-a, -b),
+            device_id_type=pl.DeviceIdType.MESH,
+        )
+        copy.start()
+        copies.append(copy)
+    for copy in copies:
+        copy.wait()
+
+
+def exchanged(lat_steps, lon_steps, pieces):
+    width = pieces[0].shape[-1]
+    flats = []
+    for piece in pieces:
+        flat = piece.reshape(-1, width)
+        flats.append(jnp.pad(flat, ((0, -flat.shape[0] % 16), (0, 0))))
+    signs = [(1, 1), (1, -1), (-1, 1), (-1, -1)]
+    in_vmem = pl.BlockSpec(memory_space=pltpu.VMEM)
+    results = pl.pallas_call(
+        functools.partial(exchange_kernel, lat_steps, lon_steps),
+        out_shape=[jax.ShapeDtypeStruct(flat.shape, flat.dtype) for flat in flats],
+        in_specs=[in_vmem] * 3,
+        out_specs=[in_vmem] * 3,
+        scratch_shapes=[pltpu.SemaphoreType.DMA((3,)), pltpu.SemaphoreType.DMA((3,))],
+        compiler_params=pltpu.CompilerParams(
+            collective_id=4 * signs.index(lat_steps) + signs.index(lon_steps),
+            has_side_effects=True,
+            vmem_limit_bytes=8 * 1024 * 1024,
+        ),
+    )(*flats)
+    return [out[: math.prod(piece.shape[:-1])].reshape(piece.shape) for out, piece in zip(results, pieces)]
 
 
 def by_segment(make, steps):
@@ -113,11 +171,10 @@
 def shift_one_way(lat_steps, lon_steps, field, lat_shift, lon_shift):
     rows = lambda step: field[:, :HALF_LAT] if step > 0 else field[:, WLAT - HALF_LAT:]
     columns = lambda part: lambda step: part[:, :, :HALF_LON] if step > 0 else part[:, :, WLON - HALF_LON:]
-    still = (0, 0)
     row_piece = by_segment(rows, lat_steps)
-    below = moved(row_piece, lat_steps, still)
-    corner = moved(by_segment(columns(row_piece), lon_steps), lat_steps, lon_steps)
-    beside = moved(by_segment(columns(field), lon_steps), still, lon_steps)
+    corner_piece = by_segment(columns(row_piece), lon_steps)
+    column_piece = by_segment(columns(field), lon_steps)
+    below, corner, beside = exchanged(lat_steps, lon_steps, (row_piece, corner_piece, column_piece))
     block_count, row_count, column_count, width = field.shape
 
     def joined(own, other, axis, start, half, size):
@@ -157,9 +214,8 @@
 
 def body(latents, land_mask, land_embed, qkv_weight, out_weight, norm_gain, offsets):
     segment_index = lax.axis_index("segment")
-    block_count, row_count, column_count, width = latents.shape
+    row_count, column_count = latents.shape[1:3]
     assert (row_count, column_count) == (WLAT, WLON)
-    total_rows = row_count * lax.axis_size("lat")
     land_term = land_mask.astype(jnp.float32)[None, :, :, None] * land_embed.astype(jnp.float32)
     seeded = (latents.astype(jnp.float32) + land_term).astype(jnp.bfloat16)
     wqkv = qkv_weight[0]
@@ -169,20 +225,14 @@
     lat_base = jnp.where(lat_offset >= HALF_LAT, lat_offset - WLAT, lat_offset)
     lon_base = jnp.where(lon_offset >= HALF_LON, lon_offset - WLON, lon_offset)
 
-    def codes_of(s):
-        held = lax.axis_index("lat") * row_count + jnp.arange(row_count, dtype=jnp.int32) + lat_base[s]
-        wrapped = (held % total_rows < lat_offset[s]).astype(jnp.int32)
-        blocks = 2 * jnp.arange(block_count, dtype=jnp.int32)
-        codes = jnp.broadcast_to(
-            blocks[:, None, None] + wrapped[None, :, None], (block_count, row_count, column_count)
-        )
-        return codes.reshape(-1)
+    def place_of(s):
+        return jnp.stack([lax.axis_index("lat") * row_count + lat_base[s], lat_offset[s]])
 
     first_in = shift(seeded, lat_base[0], lon_base[0])
-    first = attend(first_in, codes_of(0), wqkv, wout, gain)
+    first = attend(first_in, place_of(0), wqkv, wout, gain)
     passed = lax.ppermute(first, "segment", [(0, 1)])
     second_in = shift(passed, lat_base[1] - lat_base[0], lon_base[1] - lon_base[0])
-    second = attend(second_in, codes_of(1), wqkv, wout, gain)
+    second = attend(second_in, place_of(1), wqkv, wout, gain)
     merged = jnp.where(segment_index == 0, first, second)
     return shift_each(merged, -lat_base, -lon_base)[None]
 

time: 84.5 us -> 86.1 us (1.019)
  the two profiles are of different devices: /device:TPU:4 before, /device:TPU:0 now
where the time goes in v2:
time: 86.1 us; the launch traced here: 84.4 us
  Pallas kernels  46.7 us (54%)
  local copies, waits for them, and re-layouts  12 us (14%)
  between operations  7.44 us (9%)
  loops' own time  7.3 us (8%)
  other arithmetic  6.98 us (8%)
  starting transfers between devices  3.87 us (4%)
    pallas_call x3, Pallas kernels, exchanged(): pl.pallas_call(functools.partial(exchange_kernel, lat_steps, lon_steps),...  30.3 us
    pallas_call x2, Pallas kernels, attend(): pl.pallas_call(functools.partial(attend_kernel, head_size=head_size, tota...  16.5 us
    another operation x1, loops' own time, shift_each(): return lax.switch(choice, ways, field, lat_shifts[own], lon_shifts[own])  4.36 us
    ppermute x1, starting transfers between devices, body(): passed = lax.ppermute(first, 'segment', [(0, 1)])  3.87 us
    another operation x2, loops' own time, shift(): return lax.switch(choice, ways, field, lat_shift, lon_shift)  2.94 us
    another operation x2, other arithmetic, place_of(): jnp.stack([lax.axis_index('lat') * row_count + lat_base[s], lat_offset[s]])  2.56 us
  transfers between devices with their start and end apart: 1, of which 0 were waited for; matrix products, arithmetic and copies ran while one was open for 4% of the time, Pallas kernels for 0%

profile of v2, /device:TPU:0, one launch (start us, length us, event | category | flops | bytes accessed | tf_op | source)
XLA Modules:
  0.0 84.4 jit_solution(909270325275209784)
XLA Ops:
  0.0 1.0 %slice_reduce_fusion = (s32[2]{0:T(128)S(1)}, s32[2]{0:T(128)S(1)}) fusion(s32[2,2]{1,0:T(2,128)} %param.29), kind=kLoop, calls=%fused_computation.224 | loop fusion | bytes 32 | tf_op jit(solution)/shard_map/slice | solution.py:224
  1.0 1.4 %fusion.82 = (s32[1,1]{1,0:T(1,128)}, s32[1,1]{1,0:T(1,128)}) fusion(s32[2,2]{1,0:T(2,128)} %param.29), kind=kLoop, calls=%fused_computation.231 | loop fusion | bytes 16 | tf_op jit(solution)/shard_map/slice | solution.py:229
  2.3 0.7 fusion.84
  3.0 0.6 fusion.83
  3.6 0.7 convert_element_type.82
  4.3 0.7 convert_element_type.83
  6.2 0.1 broadcast_multiply_fusion
  6.3 1.0 %add_convert_fusion = bf16[2,6,12,1024]{3,2,1,0:T(8,128)(2,1)S(1)} fusion(bf16[2,6,12,1024]{3,0,2,1:T(2,128)(2,1)} %param.23, f32[6,12,1024]{2,1,0:T(8,128)S(1)} %broadcast_multiply_fusion), kind=kLoop, calls=%fused_computation.220 | loop fusion | flops 442368 | bytes 884736 | tf_op jit(solution)/shard_map/convert_element_type | solution.py:220
  7.9 15.1 %conditional.3 = (bf16[144,1024]{1,0:T(8,128)(2,1)S(1)}) conditional(s32[]{:T(128)} %clamp.11, (bf16[2,6,12,1024]{3,2,1,0:T(8,128)(2,1)S(1)}, s32[]{:T(128)}, s32[]{:T(128)}) %tuple.85, (bf16[2,6,12,1024]{3,2,1,0:T(8,128)(2,1)S(1)}, s32[]{:T(128)}, s32[]{:T(128)}) %tuple.85, (bf16[2,6,12,1024]{3,2,1,0:T(8,128)(2,1)S(1)}, ...), branch_computations={%region_0.1_spmd, %region_1.2_spmd, %region_2.3_spmd, %region_3.4_... | conditional | flops 1032200 | bytes 6176886 | solution.py:197
  8.0 0.1 slice.340
  8.1 0.1 reshape.327
  8.3 11.4 %branch_3_fun.4 = (bf16[80,1024]{1,0:T(8,128)(2,1)S(1)}, bf16[48,1024]{1,0:T(8,128)(2,1)S(1)}, bf16[80,1024]{1,0:T(8,128)(2,1)S(1)}) custom-call(bf16[80,1024]{1,0:T(8,128)(2,1)S(1)} %pad.107.below_in, bf16[48,1024]{1,0:T(8,128)(2,1)S(1)} %pad.108.corner_in, bf16[80,1024]{1,0:T(8,128)(2,1)S(1)} %pad.109.beside_in), custom_call_target="tpu_custom_call" | custom-call | tf_op jit(solution)/shard_map/cond/branch_3_fun/pallas_call | solution.py:150
  21.1 0.1 fusion.11
  21.3 0.1 reshape.330
  21.4 0.3 fusion.10
  22.8 0.1 fusion.9
  22.9 0.1 reshape.331
  23.0 0.6 constant_dynamic-slice_fusion.gain_ref
  23.6 1.3 %pad_add_fusion.1.place_ref = s32[2]{0:T(128)} fusion(s32[1]{0:T(128)} %bitcast.34, s32[1]{0:T(128)} %bitcast.33), kind=kLoop, calls=%fused_computation.227 | loop fusion | flops 2 | bytes 16 | tf_op jit(solution)/shard_map/stack | solution.py:229
  24.8 8.6 %shard_map.81 = bf16[144,1024]{1,0:T(8,128)(2,1)} custom-call(s32[2]{0:T(128)} %pad_add_fusion.1.place_ref, bf16[144,1024]{1,0:T(8,128)(2,1)S(1)} %get-tuple-element.515.x_ref, bf16[1024,3072]{1,0:T(8,128)(2,1)} %bitcast.45, bf16[1024,3072]{1,0:T(8,128)(2,1)} %bitcast.46, bf16[1024,3072]{1,0:T(8,128)(2,1)} %bitcast.47, bf16[1024,1024]{1,0:T(8,128)(2,1)} %bitcast.51, ...), custom_call_target="tpu_custom_call" | custom-call | flops 1207959552 | bytes 8388608 | tf_op jit(solution)/shard_map/pallas_call | solution.py:88
  33.4 1.0 %reshape.417 = bf16[2,6,12,1024]{3,2,1,0:T(8,128)(2,1)S(1)} reshape(bf16[144,1024]{1,0:T(8,128)(2,1)} %shard_map.81) | data formatting | bytes 589824 | tf_op jit(solution)/shard_map/reshape | solution.py:110
  34.4 3.9 %collective-permute-start = (bf16[2,6,12,1024]{3,2,1,0:T(8,128)(2,1)S(1)}, bf16[2,6,12,1024]{3,2,1,0:T(8,128)(2,1)S(1)}, u32[]{:S(2)}, u32[]{:S(2)}) collective-permute-start(bf16[2,6,12,1024]{3,2,1,0:T(8,128)(2,1)S(1)} %reshape.417), channel_id=1, source_target_pairs={{0,16},{1,17},{2,18},{3,19},{4,20},{5,21},{6,22},{7,23},{8,24},{9,... | collective-permute-start | bytes 884744 | tf_op jit(solution)/shard_map/ppermute | solution.py:233
  40.2 0.6 slice.441
  40.7 0.6 slice.443
  42.7 0.6 dynamic_slice.292
  43.3 0.6 dynamic_slice.293
  46.3 1.3 %pad_add_fusion.place_ref = s32[2]{0:T(128)} fusion(s32[1]{0:T(128)} %bitcast.29, s32[1]{0:T(128)} %bitcast.28), kind=kLoop, calls=%fused_computation.226 | loop fusion | flops 2 | bytes 16 | tf_op jit(solution)/shard_map/stack | solution.py:229
  47.6 10.1 %conditional.4 = (bf16[144,1024]{1,0:T(8,128)(2,1)S(1)}) conditional(s32[]{:T(128)} %clamp.10, (bf16[2,6,12,1024]{3,2,1,0:T(8,128)(2,1)S(1)}, s32[]{:T(128)}, s32[]{:T(128)}) %tuple.86, (bf16[2,6,12,1024]{3,2,1,0:T(8,128)(2,1)S(1)}, s32[]{:T(128)}, s32[]{:T(128)}) %tuple.86, (bf16[2,6,12,1024]{3,2,1,0:T(8,128)(2,1)S(1)}, ...), branch_computations={%region_4.5_spmd, %region_5.6_spmd, %region_6.7_spmd, %region_7.8_... | conditional | flops 1032200 | bytes 6176886 | solution.py:197
  47.7 0.1 reshape.334
  47.9 8.7 %branch_0_fun.5 = (bf16[80,1024]{1,0:T(8,128)(2,1)S(1)}, bf16[48,1024]{1,0:T(8,128)(2,1)S(1)}, bf16[80,1024]{1,0:T(8,128)(2,1)S(1)}) custom-call(bf16[80,1024]{1,0:T(8,128)(2,1)S(1)} %pad.110.below_in, bf16[48,1024]{1,0:T(8,128)(2,1)S(1)} %pad.111.corner_in, bf16[80,1024]{1,0:T(8,128)(2,1)S(1)} %pad.112.beside_in), custom_call_target="tpu_custom_call" | custom-call | tf_op jit(solution)/shard_map/cond/branch_0_fun/pallas_call | solution.py:150
  56.7 0.2 fusion.14
  56.9 0.1 reshape.335
  57.0 0.3 fusion.13
  57.3 0.2 fusion.12
  57.5 0.1 reshape.338
  57.8 7.9 %shard_map.82 = bf16[144,1024]{1,0:T(8,128)(2,1)S(1)} custom-call(s32[2]{0:T(128)} %pad_add_fusion.place_ref, bf16[144,1024]{1,0:T(8,128)(2,1)S(1)} %get-tuple-element.516.x_ref, bf16[1024,3072]{1,0:T(8,128)(2,1)} %bitcast.48, bf16[1024,3072]{1,0:T(8,128)(2,1)} %bitcast.49, bf16[1024,3072]{1,0:T(8,128)(2,1)} %bitcast.50, bf16[1024,1024]{1,0:T(8,128)(2,1)} %bitcast.52, ...), custom_call_target="tpu_custom_call" | custom-call | flops 1207959552 | bytes 8388608 | tf_op jit(solution)/shard_map/pallas_call | solution.py:88
  65.7 17.3 %conditional.5 = (bf16[1,2,6,12,1024]{4,1,3,2,0:T(2,128)(2,1)S(1)}) conditional(s32[]{:T(128)} %clamp.9, (s32[]{:T(128)}, bf16[144,1024]{1,0:T(8,128)(2,1)S(1)}, bf16[2,6,12,1024]{3,2,1,0:T(8,128)(2,1)S(1)}, s32[2]{0:T(128)S(1)}, s32[]{:T(128)}, /*index=5*/s32[2]{0:T(128)S(1)}) %tuple.87, (s32[]{:T(128)}, ...), branch_computations={%region_8.9_spmd, %region_9.10_spmd, %region_10.11_spmd, %region_1... | conditional | flops 2764819 | bytes 8020247 | solution.py:212
  65.7 0.1 reshape.360
  66.1 10.1 %branch_0_fun.6 = (bf16[80,1024]{1,0:T(8,128)(2,1)S(1)}, bf16[48,1024]{1,0:T(8,128)(2,1)S(1)}, bf16[80,1024]{1,0:T(8,128)(2,1)S(1)}) custom-call(bf16[80,1024]{1,0:T(8,128)(2,1)S(1)} %pad.122.below_in, bf16[48,1024]{1,0:T(8,128)(2,1)S(1)} %pad.123.corner_in, bf16[80,1024]{1,0:T(8,128)(2,1)S(1)} %pad.124.beside_in), custom_call_target="tpu_custom_call" | custom-call | tf_op jit(solution)/shard_map/cond/branch_0_fun/pallas_call | solution.py:150
  76.3 0.7 dynamic_slice.237
  79.1 0.2 fusion.27
  79.3 0.1 reshape.364
  79.4 0.3 fusion.26
  79.7 0.7 dynamic_slice.240
  82.4 0.2 fusion.25
  82.6 0.3 copy.20
  83.0 0.7 copy-done.2
  83.7 0.7 copy-done.1
  (46 shorter events, 0.8 us)
Async XLA Ops:
  0.0 23.0 %copy-start = (f32[2,1024]{1,0:T(2,128)S(1)}, f32[2,1024]{1,0:T(2,128)}, u32[]{:S(2)}) copy-start(f32[2,1024]{1,0:T(2,128)} %param.28) | copy-start | bytes 24580
  34.4 13.2 %collective-permute-start = (bf16[2,6,12,1024]{3,2,1,0:T(8,128)(2,1)S(1)}, bf16[2,6,12,1024]{3,2,1,0:T(8,128)(2,1)S(1)}, u32[]{:S(2)}, u32[]{:S(2)}) collective-permute-start(bf16[2,6,12,1024]{3,2,1,0:T(8,128)(2,1)S(1)} %reshape.417), channel_id=1, source_target_pairs={{0,16},{1,17},{2,18},{3,19},{4,20},{5,21},{6,22},{7,23},{8,24},{9,... | collective-permute-start | bytes 884744 | tf_op jit(solution)/shard_map/ppermute | solution.py:233
  82.9 0.7 copy-start.2
  83.7 0.7 copy-start.1

commit v3 on v2

--- a/solution.py
+++ b/solution.py
@@ -18,7 +18,11 @@
 NT = (((1,), (1,)), ((), ()))
 
 
-def cell_codes(place_ref, shape, axis, total_rows):
+def based(offset, window):
+    return jnp.where(offset >= window // 2, offset - window, offset)
+
+
+def cell_codes(base, offset, shape, axis, total_rows):
     cell = lax.broadcasted_iota(jnp.int32, shape, axis)
     line = jnp.zeros(shape, jnp.int32)
     for start in range(WLON, shape[axis], WLON):
@@ -26,22 +30,22 @@
     block = jnp.zeros(shape, jnp.int32)
     for start in range(WLAT, shape[axis] // WLON, WLAT):
         block += (line >= start).astype(jnp.int32)
-    held = place_ref[0] + line - WLAT * block
+    held = base + line - WLAT * block
     held = jnp.where(held < 0, held + total_rows, held)
     held = jnp.where(held >= total_rows, held - total_rows, held)
-    return 2 * block + (held < place_ref[1]).astype(jnp.int32)
-
-
-def attend_kernel(place_ref, x_ref, wq_ref, wk_ref, wv_ref, wo_ref, gain_ref, out_ref, total, *, head_size, total_rows):
+    return 2 * block + (held < offset).astype(jnp.int32)
+
+
+def attend_kernel(section, offsets_ref, x_ref, wq_ref, wk_ref, wv_ref, wo_ref, gain_ref, out_ref, total, *, head_size, total_rows):
     step = pl.program_id(0)
     x = x_ref[...]
     q = jnp.dot(x, wq_ref[...], preferred_element_type=jnp.float32).astype(jnp.bfloat16)
     k = jnp.dot(x, wk_ref[...], preferred_element_type=jnp.float32).astype(jnp.bfloat16)
     v = jnp.dot(x, wv_ref[...], preferred_element_type=jnp.float32).astype(jnp.bfloat16)
     cells = x.shape[0]
-    allowed = (
-        cell_codes(place_ref, (cells, 1), 0, total_rows) == cell_codes(place_ref, (1, cells), 1, total_rows)
-    )
+    offset = offsets_ref[section, 0]
+    base = lax.axis_index("lat") * WLAT + based(offset, WLAT)
+    allowed = cell_codes(base, offset, (cells, 1), 0, total_rows) == cell_codes(base, offset, (1, cells), 1, total_rows)
     scale = 1.0 / math.sqrt(head_size)
     first_half = lax.broadcasted_iota(jnp.int32, (x.shape[0], PAIR), 1) < head_size
     parts = []
@@ -72,22 +76,23 @@
     @pl.when(step == STEPS - 1)
     def _():
         whole = total[...]
+        gain = jnp.where(lax.axis_index("segment") == 0, gain_ref[0:1, :], gain_ref[1:2, :])
         centered = whole - jnp.mean(whole, axis=-1, keepdims=True)
         variance = jnp.mean(centered * centered, axis=-1, keepdims=True)
-        branch = centered * lax.rsqrt(variance + 1e-05) * gain_ref[...]
+        branch = centered * lax.rsqrt(variance + 1e-05) * gain
         out_ref[...] = (x.astype(jnp.float32) + branch).astype(jnp.bfloat16)
 
 
-def attend(field, place, wqkv, wout, gain):
+def attend(field, section, offsets, wqkv, wout, gain):
     width = field.shape[-1]
     flat = field.reshape(-1, width)
     cells = flat.shape[0]
     slab = width // STEPS
     head_size = width // HEADS
     full = lambda shape: pl.BlockSpec(shape, lambda p: (0, 0))
-    out = pl.pallas_call(
+    return pl.pallas_call(
         functools.partial(
-            attend_kernel, head_size=head_size, total_rows=WLAT * lax.axis_size("lat")
+            attend_kernel, section, head_size=head_size, total_rows=WLAT * lax.axis_size("lat")
         ),
         grid=(STEPS,),
         out_shape=jax.ShapeDtypeStruct((cells, width), jnp.bfloat16),
@@ -98,7 +103,7 @@
             pl.BlockSpec((width, slab), lambda p: (0, p + STEPS)),
             pl.BlockSpec((width, slab), lambda p: (0, p + 2 * STEPS)),
             pl.BlockSpec((slab, width), lambda p: (p, 0)),
-            full((1, width)),
+            full(gain.shape),
         ],
         out_specs=full((cells, width)),
         scratch_shapes=[pltpu.VMEM((cells, width), jnp.float32)],
@@ -106,8 +111,7 @@
         cost_estimate=pl.CostEstimate(
             flops=8 * cells * width * width, bytes_accessed=8 * width * width, transcendentals=HEADS * cells * cells
         ),
-    )(place, flat, wqkv, wqkv, wqkv, wout, gain[None, :])
-    return out.reshape(field.shape)
+    )(offsets, flat, wqkv, wqkv, wqkv, wout, gain)
 
 
 def exchange_kernel(lat_steps, lon_steps, below_in, corner_in, beside_in, below, corner, beside, send_sem, recv_sem):
@@ -168,73 +172,67 @@
     return jnp.where(lax.axis_index("segment") == 0, make(steps[0]), make(steps[1]))
 
 
-def shift_one_way(lat_steps, lon_steps, field, lat_shift, lon_shift):
+def neighbours(lat_steps, lon_steps, field):
     rows = lambda step: field[:, :HALF_LAT] if step > 0 else field[:, WLAT - HALF_LAT:]
     columns = lambda part: lambda step: part[:, :, :HALF_LON] if step > 0 else part[:, :, WLON - HALF_LON:]
     row_piece = by_segment(rows, lat_steps)
     corner_piece = by_segment(columns(row_piece), lon_steps)
     column_piece = by_segment(columns(field), lon_steps)
-    below, corner, beside = exchanged(lat_steps, lon_steps, (row_piece, corner_piece, column_piece))
-    block_count, row_count, column_count, width = field.shape
-
-    def joined(own, other, axis, start, half, size):
-        def make(step):
-            pair = [own, other] if step > 0 else [other, own]
-            return lax.dynamic_slice_in_dim(
-                jnp.concatenate(pair, axis=axis), start if step > 0 else half + start, size, axis
-            )
-
-        return make
-
-    near = by_segment(joined(field, beside, 2, lon_shift, HALF_LON, column_count), lon_steps)
-    far = by_segment(joined(below, corner, 2, lon_shift, HALF_LON, column_count), lon_steps)
-    return by_segment(joined(near, far, 1, lat_shift, HALF_LAT, row_count), lat_steps)
+    return exchanged(lat_steps, lon_steps, (row_piece, corner_piece, column_piece))
+
+
+def assembled(field, below, corner, beside, lat_shift, lon_shift):
+    near = jnp.concatenate([beside, field, beside], axis=2)
+    near = lax.dynamic_slice_in_dim(near, HALF_LON + lon_shift, field.shape[2], 2)
+    far = jnp.concatenate([corner, below, corner], axis=2)
+    far = lax.dynamic_slice_in_dim(far, HALF_LON + lon_shift, field.shape[2], 2)
+    tall = jnp.concatenate([far, near, far], axis=1)
+    return lax.dynamic_slice_in_dim(tall, HALF_LAT + lat_shift, field.shape[1], 1)
+
+
+def sign_of(lat_shift, lon_shift):
+    return 2 * (lat_shift < 0).astype(jnp.int32) + (lon_shift < 0).astype(jnp.int32)
 
 
 def shift(field, lat_shift, lon_shift):
-    choice = 2 * (lat_shift < 0).astype(jnp.int32) + (lon_shift < 0).astype(jnp.int32)
-    ways = [functools.partial(shift_one_way, (a, a), (b, b)) for a in (1, -1) for b in (1, -1)]
-    return lax.switch(choice, ways, field, lat_shift, lon_shift)
+    ways = [functools.partial(neighbours, (a, a), (b, b)) for a in (1, -1) for b in (1, -1)]
+    pieces = lax.switch(sign_of(lat_shift, lon_shift), ways, field)
+    return assembled(field, *pieces, lat_shift, lon_shift)
 
 
 def shift_each(field, lat_shifts, lon_shifts):
-    other = jnp.where((lat_shifts[1] < 0) | (lon_shifts[1] < 0), 1, 0)
-    lat_other, lon_other = lat_shifts[other], lon_shifts[other]
-    choice = 4 * other + 2 * (lat_other < 0).astype(jnp.int32) + (lon_other < 0).astype(jnp.int32)
+    signs = [sign_of(*pair) for pair in zip(lat_shifts, lon_shifts)]
+    choice = jnp.where(signs[1] > 0, 4 + signs[1], signs[0])
     ways = []
     for segment in (0, 1):
         for a in (1, -1):
             for b in (1, -1):
                 lat_steps = (a, 1) if segment == 0 else (1, a)
                 lon_steps = (b, 1) if segment == 0 else (1, b)
-                ways.append(functools.partial(shift_one_way, lat_steps, lon_steps))
-    own = lax.axis_index("segment")
-    return lax.switch(choice, ways, field, lat_shifts[own], lon_shifts[own])
+                ways.append(functools.partial(neighbours, lat_steps, lon_steps))
+    pieces = lax.switch(choice, ways, field)
+    first = lax.axis_index("segment") == 0
+    return assembled(field, *pieces, jnp.where(first, *lat_shifts), jnp.where(first, *lon_shifts))
 
 
 def body(latents, land_mask, land_embed, qkv_weight, out_weight, norm_gain, offsets):
     segment_index = lax.axis_index("segment")
-    row_count, column_count = latents.shape[1:3]
-    assert (row_count, column_count) == (WLAT, WLON)
-    land_term = land_mask.astype(jnp.float32)[None, :, :, None] * land_embed.astype(jnp.float32)
-    seeded = (latents.astype(jnp.float32) + land_term).astype(jnp.bfloat16)
+    assert latents.shape[1:3] == (WLAT, WLON)
+    embedded = latents.astype(jnp.float32) + land_embed.astype(jnp.float32)
+    seeded = jnp.where(land_mask[None, :, :, None] > 0, embedded, latents.astype(jnp.float32)).astype(jnp.bfloat16)
     wqkv = qkv_weight[0]
     wout = out_weight[0]
-    gain = lax.dynamic_index_in_dim(norm_gain, segment_index, 0, False)
-    lat_offset, lon_offset = offsets[:, 0], offsets[:, 1]
-    lat_base = jnp.where(lat_offset >= HALF_LAT, lat_offset - WLAT, lat_offset)
-    lon_base = jnp.where(lon_offset >= HALF_LON, lon_offset - WLON, lon_offset)
-
-    def place_of(s):
-        return jnp.stack([lax.axis_index("lat") * row_count + lat_base[s], lat_offset[s]])
-
+    lat_base, lon_base = [], []
+    for s in (0, 1):
+        lat_base.append(based(offsets[s, 0], WLAT))
+        lon_base.append(based(offsets[s, 1], WLON))
     first_in = shift(seeded, lat_base[0], lon_base[0])
-    first = attend(first_in, place_of(0), wqkv, wout, gain)
-    passed = lax.ppermute(first, "segment", [(0, 1)])
+    first = attend(first_in, 0, offsets, wqkv, wout, norm_gain)
+    passed = lax.ppermute(first, "segment", [(0, 1)]).reshape(latents.shape)
     second_in = shift(passed, lat_base[1] - lat_base[0], lon_base[1] - lon_base[0])
-    second = attend(second_in, place_of(1), wqkv, wout, gain)
-    merged = jnp.where(segment_index == 0, first, second)
-    return shift_each(merged, -lat_base, -lon_base)[None]
+    second = attend(second_in, 1, offsets, wqkv, wout, norm_gain)
+    merged = jnp.where(segment_index == 0, first, second).reshape(latents.shape)
+    return shift_each(merged, [-x for x in lat_base], [-x for x in lon_base])[None]
 
 
 def solution(mesh):

time: 86.1 us -> 75.8 us (0.88)
  the two profiles are of different devices: /device:TPU:0 before, /device:TPU:4 now
where the time goes in v3:
time: 75.8 us; the launch traced here: 75.5 us
  Pallas kernels  47.7 us (63%)
  between operations  8.05 us (11%)
  waiting for transfers between devices  6.41 us (8%)
  other arithmetic  6.37 us (8%)
  local copies, waits for them, and re-layouts  5.38 us (7%)
  starting transfers between devices  1.28 us (2%)
    pallas_call x3, Pallas kernels, exchanged(): pl.pallas_call(functools.partial(exchange_kernel, lat_steps, lon_steps),...  30.1 us
    pallas_call x2, Pallas kernels, attend(): pl.pallas_call(functools.partial(attend_kernel, section, head_size=head_s...  17.7 us
    ppermute x1, waiting for transfers between devices, body(): passed = lax.ppermute(first, 'segment', [(0, 1)]).reshape(latents.shape)  6.41 us
    reshape x2, local copies, waits for them, and re-layouts, attend(): flat = field.reshape(-1, width)  1.56 us
  transfers between devices with their start and end apart: 1, of which 1 were waited for; matrix products, arithmetic and copies ran while one was open for 0% of the time, Pallas kernels for 0%

profile of v3, /device:TPU:4, one launch (start us, length us, event | category | flops | bytes accessed | tf_op | source)
XLA Modules:
  0.0 75.5 jit_solution(1935700787173241549)
XLA Ops:
  0.0 1.5 %fusion.19 = (s32[1,1]{1,0:T(1,128)}, s32[1,1]{1,0:T(1,128)}, s32[1,1]{1,0:T(1,128)}, s32[1,1]{1,0:T(1,128)}) fusion(s32[2,2]{1,0:T(2,128)} %offsets_ref.3), kind=kLoop, calls=%fused_computation.62 | loop fusion | bytes 32 | tf_op jit(solution)/shard_map/slice | solution.py:228
  5.5 0.7 broadcast_compare_fusion
  6.2 0.7 convert_element_type.92
  6.9 1.2 %fusion = bf16[2,6,12,1024]{3,2,1,0:T(8,128)(2,1)S(1)} fusion(bf16[2,6,12,1024]{3,0,2,1:T(2,128)(2,1)} %param.23, f32[1024]{0:T(1024)S(1)} %convert_element_type.92, pred[6,12]{1,0:T(8,128)(4,1)S(1)} %broadcast_compare_fusion), kind=kLoop, calls=%fused_computation.13 | loop fusion | flops 589824 | bytes 593992 | tf_op jit(solution)/shard_map/convert_element_type | solution.py:222
  8.1 10.8 %conditional.3 = ((bf16[80,1024]{1,0:T(8,128)(2,1)S(1)}, bf16[48,1024]{1,0:T(8,128)(2,1)S(1)}, bf16[80,1024]{1,0:T(8,128)(2,1)S(1)})) conditional(s32[]{:T(128)} %clamp.10, bf16[2,6,12,1024]{3,2,1,0:T(8,128)(2,1)S(1)} %fusion, bf16[2,6,12,1024]{3,2,1,0:T(8,128)(2,1)S(1)} %fusion, ...), branch_computations={%region_0.1_spmd, %region_1.2_spmd, %region_2.3_spmd, %region_3.4_... | conditional | bytes 2269198 | solution.py:199
  8.2 0.1 slice.206
  8.3 0.1 reshape.209
  8.4 10.4 %branch_3_fun.3 = (bf16[80,1024]{1,0:T(8,128)(2,1)S(1)}, bf16[48,1024]{1,0:T(8,128)(2,1)S(1)}, bf16[80,1024]{1,0:T(8,128)(2,1)S(1)}) custom-call(bf16[80,1024]{1,0:T(8,128)(2,1)S(1)} %pad.107.below_in, bf16[48,1024]{1,0:T(8,128)(2,1)S(1)} %pad.108.corner_in, bf16[80,1024]{1,0:T(8,128)(2,1)S(1)} %pad.109.beside_in), custom_call_target="tpu_custom_call" | custom-call | tf_op jit(solution)/shard_map/cond/branch_3_fun/pallas_call | solution.py:154
  18.9 0.1 reshape.331
  19.1 0.4 fusion.6
  19.5 0.2 fusion.18
  19.8 0.2 fusion.12
  20.0 0.8 %reshape.273.x_ref = bf16[144,1024]{1,0:T(8,128)(2,1)} reshape(bf16[2,6,12,1024]{3,2,1,0:T(8,128)(2,1)S(1)} %fusion.12) | data formatting | bytes 589824 | tf_op jit(solution)/shard_map/reshape | solution.py:88
  20.8 8.8 %shard_map.73 = bf16[144,1024]{1,0:T(8,128)(2,1)} custom-call(s32[2,2]{1,0:T(2,128)} %offsets_ref.3, bf16[144,1024]{1,0:T(8,128)(2,1)} %reshape.273.x_ref, bf16[1024,3072]{1,0:T(8,128)(2,1)} %bitcast.9, bf16[1024,3072]{1,0:T(8,128)(2,1)} %bitcast.10, bf16[1024,3072]{1,0:T(8,128)(2,1)} %bitcast.11, bf16[1024,1024]{1,0:T(8,128)(2,1)} %bitcast.15, ...), custom_call_target="tpu_custom_call" | custom-call | flops 1207959552 | bytes 8388608 | tf_op jit(solution)/shard_map/pallas_call | solution.py:93
  29.6 1.3 %collective-permute-start = (bf16[144,1024]{1,0:T(8,128)(2,1)}, bf16[144,1024]{1,0:T(8,128)(2,1)S(1)}, u32[]{:S(2)}, u32[]{:S(2)}) collective-permute-start(bf16[144,1024]{1,0:T(8,128)(2,1)} %shard_map.73), channel_id=1, source_target_pairs={{0,16},{1,17},{2,18},{3,19},{4,20},{5,21},{6,22},{7,23},{8,24},{9,... | collective-permute-start | bytes 884744 | tf_op jit(solution)/shard_map/ppermute | solution.py:231
  34.7 6.4 %collective-permute-done = bf16[144,1024]{1,0:T(8,128)(2,1)S(1)} collective-permute-done((bf16[144,1024]{1,0:T(8,128)(2,1)}, bf16[144,1024]{1,0:T(8,128)(2,1)S(1)}, u32[]{:S(2)}, u32[]{:S(2)}) %collective-permute-start) | collective-permute-done | bytes 294944 | tf_op jit(solution)/shard_map/ppermute | solution.py:231
  41.1 0.1 reshape.274
  41.2 9.5 %conditional.4 = ((bf16[80,1024]{1,0:T(8,128)(2,1)S(1)}, bf16[48,1024]{1,0:T(8,128)(2,1)S(1)}, bf16[80,1024]{1,0:T(8,128)(2,1)S(1)})) conditional(s32[]{:T(128)} %clamp.11, bf16[2,6,12,1024]{3,2,1,0:T(8,128)(2,1)S(1)} %reshape.274, bf16[2,6,12,1024]{3,2,1,0:T(8,128)(2,1)S(1)} %reshape.274, ...), branch_computations={%region_4.5_spmd, %region_5.6_spmd, %region_6.7_spmd, %region_7.8_... | conditional | bytes 2269198 | solution.py:199
  41.3 0.1 slice.225
  41.4 0.1 reshape.226
  41.5 9.2 %branch_1_fun.4 = (bf16[80,1024]{1,0:T(8,128)(2,1)S(1)}, bf16[48,1024]{1,0:T(8,128)(2,1)S(1)}, bf16[80,1024]{1,0:T(8,128)(2,1)S(1)}) custom-call(bf16[80,1024]{1,0:T(8,128)(2,1)S(1)} %pad.113.below_in, bf16[48,1024]{1,0:T(8,128)(2,1)S(1)} %pad.114.corner_in, bf16[80,1024]{1,0:T(8,128)(2,1)S(1)} %pad.115.beside_in), custom_call_target="tpu_custom_call" | custom-call | tf_op jit(solution)/shard_map/cond/branch_1_fun/pallas_call | solution.py:154
  50.7 0.1 reshape.334
  50.9 0.4 fusion.4
  51.4 0.2 fusion.16
  51.6 0.2 fusion.10
  51.8 0.8 %reshape.278.x_ref = bf16[144,1024]{1,0:T(8,128)(2,1)} reshape(bf16[2,6,12,1024]{3,2,1,0:T(8,128)(2,1)S(1)} %fusion.10) | data formatting | bytes 589824 | tf_op jit(solution)/shard_map/reshape | solution.py:88
  52.6 0.0 copy-start
  52.6 8.8 %shard_map.74 = bf16[144,1024]{1,0:T(8,128)(2,1)} custom-call(s32[2,2]{1,0:T(2,128)} %offsets_ref.3, bf16[144,1024]{1,0:T(8,128)(2,1)} %reshape.278.x_ref, bf16[1024,3072]{1,0:T(8,128)(2,1)} %bitcast.12, bf16[1024,3072]{1,0:T(8,128)(2,1)} %bitcast.13, bf16[1024,3072]{1,0:T(8,128)(2,1)} %bitcast.14, bf16[1024,1024]{1,0:T(8,128)(2,1)} %bitcast.16, ...), custom_call_target="tpu_custom_call" | custom-call | flops 1207959552 | bytes 8388608 | tf_op jit(solution)/shard_map/pallas_call | solution.py:93
  61.5 0.0 copy-done
  61.5 1.0 %broadcast_select_fusion = bf16[144,1024]{1,0:T(8,128)(2,1)S(1)} fusion(bf16[144,1024]{1,0:T(8,128)(2,1)S(1)} %copy-done, bf16[144,1024]{1,0:T(8,128)(2,1)} %shard_map.74, pred[]{:T(512)S(6)} %eq.28), kind=kLoop, calls=%fused_computation.54 | loop fusion | flops 147456 | bytes 884737 | tf_op jit(solution)/shard_map/jit(_where)/select_n | solution.py:234
  62.5 0.1 reshape.279
  62.6 10.8 %conditional.5 = ((bf16[80,1024]{1,0:T(8,128)(2,1)S(1)}, bf16[48,1024]{1,0:T(8,128)(2,1)S(1)}, bf16[80,1024]{1,0:T(8,128)(2,1)S(1)})) conditional(s32[]{:T(128)} %clamp.9, bf16[2,6,12,1024]{3,2,1,0:T(8,128)(2,1)S(1)} %reshape.279, bf16[2,6,12,1024]{3,2,1,0:T(8,128)(2,1)S(1)} %reshape.279, ...), branch_computations={%region_8.9_spmd, %region_9.10_spmd, %region_10.11_spmd, %region_1... | conditional | flops 184324 | bytes 2637882 | solution.py:213
  62.7 0.1 reshape.253
  62.9 10.5 %branch_6_fun.1 = (bf16[80,1024]{1,0:T(8,128)(2,1)S(1)}, bf16[48,1024]{1,0:T(8,128)(2,1)S(1)}, bf16[80,1024]{1,0:T(8,128)(2,1)S(1)}) custom-call(bf16[80,1024]{1,0:T(8,128)(2,1)S(1)} %pad.140.below_in, bf16[48,1024]{1,0:T(8,128)(2,1)S(1)} %pad.141.corner_in, bf16[80,1024]{1,0:T(8,128)(2,1)S(1)} %pad.142.beside_in), custom_call_target="tpu_custom_call" | custom-call | tf_op jit(solution)/shard_map/cond/branch_6_fun/pallas_call | solution.py:154
  73.4 0.1 reshape.337
  73.6 0.4 fusion.2
  74.0 0.2 fusion.14
  74.3 0.2 fusion.8
  74.5 1.0 %copy.15 = bf16[2,6,12,1024]{3,0,2,1:T(2,128)(2,1)} copy(bf16[2,6,12,1024]{3,2,1,0:T(8,128)(2,1)S(1)} %fusion.8) | data formatting | bytes 589824 | tf_op jit(solution)/shard_map/dynamic_slice | solution.py:190
  (37 shorter events, 0.7 us)
Async XLA Ops:
  29.6 11.5 %collective-permute-start = (bf16[144,1024]{1,0:T(8,128)(2,1)}, bf16[144,1024]{1,0:T(8,128)(2,1)S(1)}, u32[]{:S(2)}, u32[]{:S(2)}) collective-permute-start(bf16[144,1024]{1,0:T(8,128)(2,1)} %shard_map.73), channel_id=1, source_target_pairs={{0,16},{1,17},{2,18},{3,19},{4,20},{5,21},{6,22},{7,23},{8,24},{9,... | collective-permute-start | bytes 884744 | tf_op jit(solution)/shard_map/ppermute | solution.py:231
  52.6 8.9 %copy-start = (bf16[144,1024]{1,0:T(8,128)(2,1)S(1)}, bf16[144,1024]{1,0:T(8,128)(2,1)}, u32[]{:S(2)}) copy-start(bf16[144,1024]{1,0:T(8,128)(2,1)} %shard_map.73) | copy-start | bytes 884740

commit v4 on v3

--- a/solution.py
+++ b/solution.py
@@ -15,6 +15,7 @@
 HALF_LON = WLON // 2
 STEPS = 4
 PAIR = 128
+CHUNK = 48
 NT = (((1,), (1,)), ((), ()))
 
 
@@ -36,15 +37,39 @@
     return 2 * block + (held < offset).astype(jnp.int32)
 
 
-def attend_kernel(section, offsets_ref, x_ref, wq_ref, wk_ref, wv_ref, wo_ref, gain_ref, out_ref, total, *, head_size, total_rows):
+def attend_kernel(section, offsets_ref, x_ref, wq_ref, wk_ref, wv_ref, wo_ref, gain_ref, out_ref, *rest, head_size, total_rows, hop):
+    if hop:
+        passed_ref, total, staged, send_sem, recv_sem, local_sem = rest
+    else:
+        (total,) = rest
     step = pl.program_id(0)
+    segment, lon, lat = (lax.axis_index(axis) for axis in ("segment", "lon", "lat"))
+    if hop:
+        barrier = pltpu.get_barrier_semaphore()
+        partner = (1 - segment, lon, lat)
+
+        @pl.when((step == 0) & (segment == 1))
+        def _():
+            pl.semaphore_signal(barrier, inc=1, device_id=partner, device_id_type=pl.DeviceIdType.MESH)
+
+        def hop_copy(index):
+            rows = pl.ds(index * CHUNK, CHUNK)
+            return pltpu.make_async_remote_copy(
+                src_ref=staged.at[rows],
+                dst_ref=passed_ref.at[rows],
+                send_sem=send_sem.at[index],
+                recv_sem=recv_sem.at[index],
+                device_id=partner,
+                device_id_type=pl.DeviceIdType.MESH,
+            )
+
     x = x_ref[...]
     q = jnp.dot(x, wq_ref[...], preferred_element_type=jnp.float32).astype(jnp.bfloat16)
     k = jnp.dot(x, wk_ref[...], preferred_element_type=jnp.float32).astype(jnp.bfloat16)
     v = jnp.dot(x, wv_ref[...], preferred_element_type=jnp.float32).astype(jnp.bfloat16)
     cells = x.shape[0]
     offset = offsets_ref[section, 0]
-    base = lax.axis_index("lat") * WLAT + based(offset, WLAT)
+    base = lat * WLAT + based(offset, WLAT)
     allowed = cell_codes(base, offset, (cells, 1), 0, total_rows) == cell_codes(base, offset, (1, cells), 1, total_rows)
     scale = 1.0 / math.sqrt(head_size)
     first_half = lax.broadcasted_iota(jnp.int32, (x.shape[0], PAIR), 1) < head_size
@@ -75,27 +100,66 @@
 
     @pl.when(step == STEPS - 1)
     def _():
-        whole = total[...]
-        gain = jnp.where(lax.axis_index("segment") == 0, gain_ref[0:1, :], gain_ref[1:2, :])
-        centered = whole - jnp.mean(whole, axis=-1, keepdims=True)
-        variance = jnp.mean(centered * centered, axis=-1, keepdims=True)
-        branch = centered * lax.rsqrt(variance + 1e-05) * gain
-        out_ref[...] = (x.astype(jnp.float32) + branch).astype(jnp.bfloat16)
+        if hop:
+
+            @pl.when(segment == 0)
+            def _():
+                pl.semaphore_wait(barrier, 1)
+
+        gain = jnp.where(segment == 0, gain_ref[0:1, :], gain_ref[1:2, :])
+        chunks = cells // CHUNK
+        for index in range(chunks):
+            rows = pl.ds(index * CHUNK, CHUNK)
+            whole = total[rows, :]
+            centered = whole - jnp.mean(whole, axis=-1, keepdims=True)
+            variance = jnp.mean(centered * centered, axis=-1, keepdims=True)
+            branch = centered * lax.rsqrt(variance + 1e-05) * gain
+            summed = (x_ref[rows, :].astype(jnp.float32) + branch).astype(jnp.bfloat16)
+            out_ref[rows, :] = summed
+            if hop:
+                staged[rows, :] = summed
+
+                @pl.when(segment == 0)
+                def _():
+                    hop_copy(index).start()
+
+        if hop:
+
+            @pl.when(segment == 0)
+            def _():
+                kept = pltpu.make_async_copy(staged, passed_ref, local_sem)
+                kept.start()
+                for index in range(chunks):
+                    hop_copy(index).wait_send()
+                kept.wait()
+
+            @pl.when(segment == 1)
+            def _():
+                for index in range(chunks):
+                    hop_copy(index).wait_recv()
 
 
 def attend(field, section, offsets, wqkv, wout, gain):
+    hop = section == 0
     width = field.shape[-1]
     flat = field.reshape(-1, width)
     cells = flat.shape[0]
+    assert cells % CHUNK == 0
     slab = width // STEPS
     head_size = width // HEADS
+    hop_scratch = [
+        pltpu.VMEM((cells, width), jnp.bfloat16),
+        pltpu.SemaphoreType.DMA((cells // CHUNK,)),
+        pltpu.SemaphoreType.DMA((cells // CHUNK,)),
+        pltpu.SemaphoreType.DMA,
+    ]
     full = lambda shape: pl.BlockSpec(shape, lambda p: (0, 0))
     return pl.pallas_call(
         functools.partial(
-            attend_kernel, section, head_size=head_size, total_rows=WLAT * lax.axis_size("lat")
+            attend_kernel, section, head_size=head_size, total_rows=WLAT * lax.axis_size("lat"), hop=hop
         ),
         grid=(STEPS,),
-        out_shape=jax.ShapeDtypeStruct((cells, width), jnp.bfloat16),
+        out_shape=[jax.ShapeDtypeStruct((cells, width), jnp.bfloat16)] * (2 if hop else 1),
         in_specs=[
             pl.BlockSpec(memory_space=pltpu.SMEM),
             full((cells, width)),
@@ -105,9 +169,13 @@
             pl.BlockSpec((slab, width), lambda p: (p, 0)),
             full(gain.shape),
         ],
-        out_specs=full((cells, width)),
-        scratch_shapes=[pltpu.VMEM((cells, width), jnp.float32)],
-        compiler_params=pltpu.CompilerParams(vmem_limit_bytes=56 * 1024 * 1024),
+        out_specs=[full((cells, width))] + ([pl.BlockSpec(memory_space=pl.ANY)] if hop else []),
+        scratch_shapes=[pltpu.VMEM((cells, width), jnp.float32)] + (hop_scratch if hop else []),
+        compiler_params=pltpu.CompilerParams(
+            vmem_limit_bytes=56 * 1024 * 1024,
+            collective_id=16 if hop else None,
+            has_side_effects=hop,
+        ),
         cost_estimate=pl.CostEstimate(
             flops=8 * cells * width * width, bytes_accessed=8 * width * width, transcendentals=HEADS * cells * cells
         ),
@@ -227,10 +295,10 @@
         lat_base.append(based(offsets[s, 0], WLAT))
         lon_base.append(based(offsets[s, 1], WLON))
     first_in = shift(seeded, lat_base[0], lon_base[0])
-    first = attend(first_in, 0, offsets, wqkv, wout, norm_gain)
-    passed = lax.ppermute(first, "segment", [(0, 1)]).reshape(latents.shape)
+    first, passed = attend(first_in, 0, offsets, wqkv, wout, norm_gain)
+    passed = passed.reshape(latents.shape)
     second_in = shift(passed, lat_base[1] - lat_base[0], lon_base[1] - lon_base[0])
-    second = attend(second_in, 1, offsets, wqkv, wout, norm_gain)
+    (second,) = attend(second_in, 1, offsets, wqkv, wout, norm_gain)
     merged = jnp.where(segment_index == 0, first, second).reshape(latents.shape)
     return shift_each(merged, [-x for x in lat_base], [-x for x in lon_base])[None]
 

time: 75.8 us -> 77.3 us (1.020)
  Pallas kernels: 47.7 us -> 55.6 us
  waiting for transfers between devices: 6.41 us -> 0 us
  starting transfers between devices: 1.28 us -> 0 us
  local copies, waits for them, and re-layouts: 5.38 us -> 6.35 us
    pallas_call x2, Pallas kernels: 17.7 us -> 25.7 us  [attend(): pl.pallas_call(functools.partial(attend_kernel, section, head_size=head_s...]
    ppermute x1 -> x0, waiting for transfers between devices: 6.41 us -> none  [body(): passed = lax.ppermute(first, 'segment', [(0, 1)]).reshape(latents.shape)]
    ppermute x1 -> x0, starting transfers between devices: 1.28 us -> none  [body(): passed = lax.ppermute(first, 'segment', [(0, 1)]).reshape(latents.shape)]
    reshape x1, local copies, waits for them, and re-layouts: 0.07 us -> 1.03 us  [body(): passed = passed.reshape(latents.shape)]
  transfers between devices with their start and end apart: 1 -> 0, of which waited for: 1 -> 0; matrix products, arithmetic and copies ran while one was open for 0% -> 0% of each run, Pallas kernels for 0% -> 0%
where the time goes in v4:
time: 77.3 us; the launch traced here: 76.8 us
  Pallas kernels  55.6 us (72%)
  between operations  8.09 us (10%)
  other arithmetic  6.35 us (8%)
  local copies, waits for them, and re-layouts  6.35 us (8%)
    pallas_call x3, Pallas kernels, exchanged(): pl.pallas_call(functools.partial(exchange_kernel, lat_steps, lon_steps),...  29.9 us
    pallas_call x2, Pallas kernels, attend(): pl.pallas_call(functools.partial(attend_kernel, section, head_size=head_s...  25.7 us
    reshape x2, local copies, waits for them, and re-layouts, attend(): flat = field.reshape(-1, width)  1.56 us

profile of v4, /device:TPU:4, one launch (start us, length us, event | category | flops | bytes accessed | tf_op | source)
XLA Modules:
  0.0 76.8 jit_solution(2797614182109095831)
XLA Ops:
  0.0 0.7 broadcast_compare_fusion
  0.7 1.5 %fusion.19 = (s32[1,1]{1,0:T(1,128)}, s32[1,1]{1,0:T(1,128)}, s32[1,1]{1,0:T(1,128)}, s32[1,1]{1,0:T(1,128)}) fusion(s32[2,2]{1,0:T(2,128)} %offsets_ref.3), kind=kLoop, calls=%fused_computation.62 | loop fusion | bytes 32 | tf_op jit(solution)/shard_map/slice | solution.py:296
  10.0 0.7 convert_element_type.92
  10.7 1.2 %fusion = bf16[2,6,12,1024]{3,2,1,0:T(8,128)(2,1)S(1)} fusion(bf16[2,6,12,1024]{3,0,2,1:T(2,128)(2,1)} %param.23, f32[1024]{0:T(1024)S(1)} %convert_element_type.92, pred[6,12]{1,0:T(8,128)(4,1)S(1)} %broadcast_compare_fusion), kind=kLoop, calls=%fused_computation.13 | loop fusion | flops 589824 | bytes 593992 | tf_op jit(solution)/shard_map/convert_element_type | solution.py:290
  11.9 10.8 %conditional.3 = ((bf16[80,1024]{1,0:T(8,128)(2,1)S(1)}, bf16[48,1024]{1,0:T(8,128)(2,1)S(1)}, bf16[80,1024]{1,0:T(8,128)(2,1)S(1)})) conditional(s32[]{:T(128)} %clamp.10, bf16[2,6,12,1024]{3,2,1,0:T(8,128)(2,1)S(1)} %fusion, bf16[2,6,12,1024]{3,2,1,0:T(8,128)(2,1)S(1)} %fusion, ...), branch_computations={%region_0.1_spmd, %region_1.2_spmd, %region_2.3_spmd, %region_3.4_... | conditional | bytes 2269198 | solution.py:267
  12.0 0.1 slice.206
  12.2 0.1 reshape.209
  12.3 10.4 %branch_3_fun.3 = (bf16[80,1024]{1,0:T(8,128)(2,1)S(1)}, bf16[48,1024]{1,0:T(8,128)(2,1)S(1)}, bf16[80,1024]{1,0:T(8,128)(2,1)S(1)}) custom-call(bf16[80,1024]{1,0:T(8,128)(2,1)S(1)} %pad.107.below_in, bf16[48,1024]{1,0:T(8,128)(2,1)S(1)} %pad.108.corner_in, bf16[80,1024]{1,0:T(8,128)(2,1)S(1)} %pad.109.beside_in), custom_call_target="tpu_custom_call" | custom-call | tf_op jit(solution)/shard_map/cond/branch_3_fun/pallas_call | solution.py:222
  22.7 0.1 reshape.331
  22.8 0.4 fusion.6
  23.4 0.2 fusion.18
  23.6 0.2 fusion.12
  23.9 0.8 %reshape.273.x_ref = bf16[144,1024]{1,0:T(8,128)(2,1)} reshape(bf16[2,6,12,1024]{3,2,1,0:T(8,128)(2,1)S(1)} %fusion.12) | data formatting | bytes 589824 | tf_op jit(solution)/shard_map/reshape | solution.py:145
  24.6 16.9 %shard_map.73 = (bf16[144,1024]{1,0:T(8,128)(2,1)}, bf16[144,1024]{1,0:T(8,128)(2,1)}) custom-call(s32[2,2]{1,0:T(2,128)} %offsets_ref.3, bf16[144,1024]{1,0:T(8,128)(2,1)} %reshape.273.x_ref, bf16[1024,3072]{1,0:T(8,128)(2,1)} %bitcast.9, bf16[1024,3072]{1,0:T(8,128)(2,1)} %bitcast.10, bf16[1024,3072]{1,0:T(8,128)(2,1)} %bitcast.11, ...), custom_call_target="tpu_custom_call" | custom-call | flops 1207959552 | bytes 8388608 | tf_op jit(solution)/shard_map/pallas_call | solution.py:157
  41.5 1.0 %reshape.274 = bf16[2,6,12,1024]{3,2,1,0:T(8,128)(2,1)S(1)} reshape(bf16[144,1024]{1,0:T(8,128)(2,1)} %get-tuple-element.39) | data formatting | bytes 589824 | tf_op jit(solution)/shard_map/reshape | solution.py:299
  42.6 11.2 %conditional.4 = ((bf16[80,1024]{1,0:T(8,128)(2,1)S(1)}, bf16[48,1024]{1,0:T(8,128)(2,1)S(1)}, bf16[80,1024]{1,0:T(8,128)(2,1)S(1)})) conditional(s32[]{:T(128)} %clamp.11, bf16[2,6,12,1024]{3,2,1,0:T(8,128)(2,1)S(1)} %reshape.274, bf16[2,6,12,1024]{3,2,1,0:T(8,128)(2,1)S(1)} %reshape.274, ...), branch_computations={%region_4.5_spmd, %region_5.6_spmd, %region_6.7_spmd, %region_7.8_... | conditional | bytes 2269198 | solution.py:267
  42.7 0.1 slice.231
  42.8 0.1 reshape.232
  42.9 10.8 %branch_3_fun.4 = (bf16[80,1024]{1,0:T(8,128)(2,1)S(1)}, bf16[48,1024]{1,0:T(8,128)(2,1)S(1)}, bf16[80,1024]{1,0:T(8,128)(2,1)S(1)}) custom-call(bf16[80,1024]{1,0:T(8,128)(2,1)S(1)} %pad.119.below_in, bf16[48,1024]{1,0:T(8,128)(2,1)S(1)} %pad.120.corner_in, bf16[80,1024]{1,0:T(8,128)(2,1)S(1)} %pad.121.beside_in), custom_call_target="tpu_custom_call" | custom-call | tf_op jit(solution)/shard_map/cond/branch_3_fun/pallas_call | solution.py:222
  53.8 0.1 reshape.334
  53.8 0.4 fusion.4
  54.4 0.2 fusion.16
  54.6 0.2 fusion.10
  54.9 0.8 %reshape.278.x_ref = bf16[144,1024]{1,0:T(8,128)(2,1)} reshape(bf16[2,6,12,1024]{3,2,1,0:T(8,128)(2,1)S(1)} %fusion.10) | data formatting | bytes 589824 | tf_op jit(solution)/shard_map/reshape | solution.py:145
  55.7 0.0 copy-start
  55.7 8.8 %shard_map.74 = bf16[144,1024]{1,0:T(8,128)(2,1)} custom-call(s32[2,2]{1,0:T(2,128)} %offsets_ref.3, bf16[144,1024]{1,0:T(8,128)(2,1)} %reshape.278.x_ref, bf16[1024,3072]{1,0:T(8,128)(2,1)} %bitcast.12, bf16[1024,3072]{1,0:T(8,128)(2,1)} %bitcast.13, bf16[1024,3072]{1,0:T(8,128)(2,1)} %bitcast.14, bf16[1024,1024]{1,0:T(8,128)(2,1)} %bitcast.16, ...), custom_call_target="tpu_custom_call" | custom-call | flops 1207959552 | bytes 8388608 | tf_op jit(solution)/shard_map/pallas_call | solution.py:157
  64.5 0.0 copy-done
  64.5 1.0 %broadcast_select_fusion = bf16[144,1024]{1,0:T(8,128)(2,1)S(1)} fusion(bf16[144,1024]{1,0:T(8,128)(2,1)S(1)} %copy-done, bf16[144,1024]{1,0:T(8,128)(2,1)} %shard_map.74, pred[]{:T(512)S(6)} %eq.28), kind=kLoop, calls=%fused_computation.54 | loop fusion | flops 147456 | bytes 884737 | tf_op jit(solution)/shard_map/jit(_where)/select_n | solution.py:302
  65.5 0.1 reshape.279
  65.6 9.0 %conditional.5 = ((bf16[80,1024]{1,0:T(8,128)(2,1)S(1)}, bf16[48,1024]{1,0:T(8,128)(2,1)S(1)}, bf16[80,1024]{1,0:T(8,128)(2,1)S(1)})) conditional(s32[]{:T(128)} %clamp.9, bf16[2,6,12,1024]{3,2,1,0:T(8,128)(2,1)S(1)} %reshape.279, bf16[2,6,12,1024]{3,2,1,0:T(8,128)(2,1)S(1)} %reshape.279, ...), branch_computations={%region_8.9_spmd, %region_9.10_spmd, %region_10.11_spmd, %region_1... | conditional | flops 184324 | bytes 2637882 | solution.py:281
  65.8 0.1 reshape.235
  65.9 8.7 %branch_0_fun.5 = (bf16[80,1024]{1,0:T(8,128)(2,1)S(1)}, bf16[48,1024]{1,0:T(8,128)(2,1)S(1)}, bf16[80,1024]{1,0:T(8,128)(2,1)S(1)}) custom-call(bf16[80,1024]{1,0:T(8,128)(2,1)S(1)} %pad.122.below_in, bf16[48,1024]{1,0:T(8,128)(2,1)S(1)} %pad.123.corner_in, bf16[80,1024]{1,0:T(8,128)(2,1)S(1)} %pad.124.beside_in), custom_call_target="tpu_custom_call" | custom-call | tf_op jit(solution)/shard_map/cond/branch_0_fun/pallas_call | solution.py:222
  74.6 0.1 reshape.337
  74.7 0.4 fusion.2
  75.3 0.2 fusion.14
  75.5 0.2 fusion.8
  75.7 1.0 %copy.15 = bf16[2,6,12,1024]{3,0,2,1:T(2,128)(2,1)} copy(bf16[2,6,12,1024]{3,2,1,0:T(8,128)(2,1)S(1)} %fusion.8) | data formatting | bytes 589824 | tf_op jit(solution)/shard_map/dynamic_slice | solution.py:258
  (37 shorter events, 0.7 us)
Async XLA Ops:
  55.7 8.8 %copy-start = (bf16[144,1024]{1,0:T(8,128)(2,1)S(1)}, bf16[144,1024]{1,0:T(8,128)(2,1)}, u32[]{:S(2)}) copy-start(bf16[144,1024]{1,0:T(8,128)(2,1)} %get-tuple-element.38) | copy-start | bytes 884740

commit v5 on v4

--- a/solution.py
+++ b/solution.py
@@ -249,28 +249,59 @@
     return exchanged(lat_steps, lon_steps, (row_piece, corner_piece, column_piece))
 
 
-def assembled(field, below, corner, beside, lat_shift, lon_shift):
+def assembled(field, below, corner, beside, row, column):
+    sliced = functools.partial(lax.dynamic_slice_in_dim, allow_negative_indices=False)
     near = jnp.concatenate([beside, field, beside], axis=2)
-    near = lax.dynamic_slice_in_dim(near, HALF_LON + lon_shift, field.shape[2], 2)
+    near = sliced(near, column, field.shape[2], 2)
     far = jnp.concatenate([corner, below, corner], axis=2)
-    far = lax.dynamic_slice_in_dim(far, HALF_LON + lon_shift, field.shape[2], 2)
+    far = sliced(far, column, field.shape[2], 2)
     tall = jnp.concatenate([far, near, far], axis=1)
-    return lax.dynamic_slice_in_dim(tall, HALF_LAT + lat_shift, field.shape[1], 1)
+    return sliced(tall, row, field.shape[1], 1)
 
 
 def sign_of(lat_shift, lon_shift):
-    return 2 * (lat_shift < 0).astype(jnp.int32) + (lon_shift < 0).astype(jnp.int32)
-
-
-def shift(field, lat_shift, lon_shift):
+    return jnp.where(lat_shift < 0, 2, 0) + jnp.where(lon_shift < 0, 1, 0)
+
+
+def plan_kernel(offsets_ref, *outs):
+    lat_base = [based(offsets_ref[s, 0], WLAT) for s in (0, 1)]
+    lon_base = [based(offsets_ref[s, 1], WLON) for s in (0, 1)]
+    first = lax.axis_index("segment") == 0
+    lat_step, lon_step = lat_base[1] - lat_base[0], lon_base[1] - lon_base[0]
+    back = [sign_of(-lat_base[s], -lon_base[s]) for s in (0, 1)]
+    numbers = (
+        sign_of(lat_base[0], lon_base[0]),
+        HALF_LAT + lat_base[0],
+        HALF_LON + lon_base[0],
+        sign_of(lat_step, lon_step),
+        HALF_LAT + lat_step,
+        HALF_LON + lon_step,
+        jnp.where(back[1] > 0, 4 + back[1], back[0]),
+        HALF_LAT - jnp.where(first, lat_base[0], lat_base[1]),
+        HALF_LON - jnp.where(first, lon_base[0], lon_base[1]),
+    )
+    for out, number in zip(outs, numbers):
+        out[0] = number
+
+
+def planned(offsets):
+    in_smem = pl.BlockSpec(memory_space=pltpu.SMEM)
+    numbers = pl.pallas_call(
+        plan_kernel,
+        out_shape=[jax.ShapeDtypeStruct((1,), jnp.int32)] * 9,
+        in_specs=[in_smem],
+        out_specs=[in_smem] * 9,
+    )(offsets)
+    numbers = [number.reshape(()) for number in numbers]
+    return numbers[:3], numbers[3:6], numbers[6:]
+
+
+def shift(field, choice, row, column):
     ways = [functools.partial(neighbours, (a, a), (b, b)) for a in (1, -1) for b in (1, -1)]
-    pieces = lax.switch(sign_of(lat_shift, lon_shift), ways, field)
-    return assembled(field, *pieces, lat_shift, lon_shift)
-
-
-def shift_each(field, lat_shifts, lon_shifts):
-    signs = [sign_of(*pair) for pair in zip(lat_shifts, lon_shifts)]
-    choice = jnp.where(signs[1] > 0, 4 + signs[1], signs[0])
+    return assembled(field, *lax.switch(choice, ways, field), row, column)
+
+
+def shift_each(field, choice, row, column):
     ways = []
     for segment in (0, 1):
         for a in (1, -1):
@@ -278,9 +309,7 @@
                 lat_steps = (a, 1) if segment == 0 else (1, a)
                 lon_steps = (b, 1) if segment == 0 else (1, b)
                 ways.append(functools.partial(neighbours, lat_steps, lon_steps))
-    pieces = lax.switch(choice, ways, field)
-    first = lax.axis_index("segment") == 0
-    return assembled(field, *pieces, jnp.where(first, *lat_shifts), jnp.where(first, *lon_shifts))
+    return assembled(field, *lax.switch(choice, ways, field), row, column)
 
 
 def body(latents, land_mask, land_embed, qkv_weight, out_weight, norm_gain, offsets):
@@ -290,17 +319,14 @@
     seeded = jnp.where(land_mask[None, :, :, None] > 0, embedded, latents.astype(jnp.float32)).astype(jnp.bfloat16)
     wqkv = qkv_weight[0]
     wout = out_weight[0]
-    lat_base, lon_base = [], []
-    for s in (0, 1):
-        lat_base.append(based(offsets[s, 0], WLAT))
-        lon_base.append(based(offsets[s, 1], WLON))
-    first_in = shift(seeded, lat_base[0], lon_base[0])
+    into_first, into_second, back = planned(offsets)
+    first_in = shift(seeded, *into_first)
     first, passed = attend(first_in, 0, offsets, wqkv, wout, norm_gain)
     passed = passed.reshape(latents.shape)
-    second_in = shift(passed, lat_base[1] - lat_base[0], lon_base[1] - lon_base[0])
+    second_in = shift(passed, *into_second)
     (second,) = attend(second_in, 1, offsets, wqkv, wout, norm_gain)
     merged = jnp.where(segment_index == 0, first, second).reshape(latents.shape)
-    return shift_each(merged, [-x for x in lat_base], [-x for x in lon_base])[None]
+    return shift_each(merged, *back)[None]
 
 
 def solution(mesh):

time: 77.3 us -> 76.9 us (level)
  between operations: 8.09 us -> 2.18 us
  other arithmetic: 6.35 us -> 12.1 us
  local copies, waits for them, and re-layouts: 6.35 us -> 4.76 us
  Pallas kernels: 55.6 us -> 56.9 us
    concatenate x3, other arithmetic: 0.72 us -> 2.64 us  [assembled(): tall = jnp.concatenate([far, near, far], axis=1)]
    concatenate x3, other arithmetic: 0.7 us -> 2.54 us  [assembled(): far = jnp.concatenate([corner, below, corner], axis=2)]
    concatenate x3, other arithmetic: 1.34 us -> 3.18 us  [assembled(): near = jnp.concatenate([beside, field, beside], axis=2)]
    slice x1 -> x0, local copies, waits for them, and re-layouts: 1.48 us -> none  [body(): lon_base.append(based(offsets[s, 1], WLON))]
    pallas_call x0 -> x1, Pallas kernels: none -> 1.28 us  [planned(): pl.pallas_call(plan_kernel, out_shape=[jax.ShapeDtypeStruct((1,), jnp.int...]
where the time goes in v5:
time: 76.9 us; the launch traced here: 76.3 us
  Pallas kernels  56.9 us (74%)
  other arithmetic  12.1 us (16%)
  local copies, waits for them, and re-layouts  4.76 us (6%)
  between operations  2.18 us (3%)
    pallas_call x3, Pallas kernels, exchanged(): pl.pallas_call(functools.partial(exchange_kernel, lat_steps, lon_steps),...  29.9 us
    pallas_call x2, Pallas kernels, attend(): pl.pallas_call(functools.partial(attend_kernel, section, head_size=head_s...  25.7 us
    concatenate x3, other arithmetic, assembled(): near = jnp.concatenate([beside, field, beside], axis=2)  3.18 us
    concatenate x3, other arithmetic, assembled(): tall = jnp.concatenate([far, near, far], axis=1)  2.64 us
    concatenate x3, other arithmetic, assembled(): far = jnp.concatenate([corner, below, corner], axis=2)  2.54 us
    reshape x2, local copies, waits for them, and re-layouts, attend(): flat = field.reshape(-1, width)  1.56 us

profile of v5, /device:TPU:4, one launch (start us, length us, event | category | flops | bytes accessed | tf_op | source)
XLA Modules:
  0.0 76.3 jit_solution(7250703404169822259)
XLA Ops:
  0.0 1.3 %shard_map.73 = (s32[1]{0:T(128)}, s32[1]{0:T(128)}, s32[1]{0:T(128)}, s32[1]{0:T(128)}, s32[1]{0:T(128)}, /*index=5*/s32[1]{0:T(128)}, s32[1]{0:T(128)}, s32[1]{0:T(128)}, s32[1]{0:T(128)}) custom-call(s32[2,2]{1,0:T(2,128)} %offsets_ref.5), custom_call_target="tpu_custom_call" | custom-call | tf_op jit(solution)/shard_map/pallas_call | solution.py:289
  2.6 0.7 convert_element_type.73
  3.3 0.7 broadcast_compare_fusion
  3.9 1.2 %fusion = bf16[2,6,12,1024]{3,2,1,0:T(8,128)(2,1)S(1)} fusion(bf16[2,6,12,1024]{3,0,2,1:T(2,128)(2,1)} %param.23, f32[1024]{0:T(1024)S(1)} %convert_element_type.73, pred[6,12]{1,0:T(8,128)(4,1)S(1)} %broadcast_compare_fusion), kind=kLoop, calls=%fused_computation.13 | loop fusion | flops 589824 | bytes 593992 | tf_op jit(solution)/shard_map/convert_element_type | solution.py:319
  5.2 10.8 %conditional.3 = ((bf16[80,1024]{1,0:T(8,128)(2,1)S(1)}, bf16[48,1024]{1,0:T(8,128)(2,1)S(1)}, bf16[80,1024]{1,0:T(8,128)(2,1)S(1)})) conditional(s32[]{:T(128)} %bitcast.1, bf16[2,6,12,1024]{3,2,1,0:T(8,128)(2,1)S(1)} %fusion, bf16[2,6,12,1024]{3,2,1,0:T(8,128)(2,1)S(1)} %fusion, ...), branch_computations={%region_0.1_spmd, %region_1.2_spmd, %region_2.3_spmd, %region_3.4_... | conditional | bytes 2269198 | solution.py:301
  5.4 0.1 slice.202
  5.5 0.1 reshape.244
  5.5 10.4 %branch_3_fun.3 = (bf16[80,1024]{1,0:T(8,128)(2,1)S(1)}, bf16[48,1024]{1,0:T(8,128)(2,1)S(1)}, bf16[80,1024]{1,0:T(8,128)(2,1)S(1)}) custom-call(bf16[80,1024]{1,0:T(8,128)(2,1)S(1)} %pad.107.below_in, bf16[48,1024]{1,0:T(8,128)(2,1)S(1)} %pad.108.corner_in, bf16[80,1024]{1,0:T(8,128)(2,1)S(1)} %pad.109.beside_in), custom_call_target="tpu_custom_call" | custom-call | tf_op jit(solution)/shard_map/cond/branch_3_fun/pallas_call | solution.py:222
  16.1 0.9 %fusion.18 = bf16[2,3,12,1024]{3,2,1,0:T(8,128)(2,1)S(1)} fusion(s32[]{:T(128)} %bitcast.2, bf16[2,3,6,1024]{3,2,1,0:T(8,128)(2,1)S(1)} %reshape.369, bf16[2,3,12,1024]{3,2,1,0:T(8,128)(2,1)S(1)} %reshape.368), kind=kLoop, calls=%fused_computation.60 | loop fusion | flops 442368 | bytes 368644 | tf_op jit(solution)/shard_map/concatenate | solution.py:256
  17.0 0.1 reshape.367
  17.0 1.1 %fusion.6 = bf16[2,6,12,1024]{3,2,1,0:T(8,128)(2,1)S(1)} fusion(s32[]{:T(128)} %bitcast.2, bf16[2,6,6,1024]{3,2,1,0:T(8,128)(2,1)S(1)} %reshape.367, bf16[2,6,12,1024]{3,2,1,0:T(8,128)(2,1)S(1)} %fusion), kind=kLoop, calls=%fused_computation.37 | loop fusion | flops 884736 | bytes 737284 | tf_op jit(solution)/shard_map/concatenate | solution.py:254
  18.1 0.9 %fusion.12 = bf16[2,6,12,1024]{3,2,1,0:T(8,128)(2,1)S(1)} fusion(s32[]{:T(128)} %bitcast.3, bf16[2,3,12,1024]{3,2,1,0:T(8,128)(2,1)S(1)} %fusion.18, bf16[2,6,12,1024]{3,2,1,0:T(8,128)(2,1)S(1)} %fusion.6), kind=kLoop, calls=%fused_computation.43 | loop fusion | flops 294912 | bytes 737284 | tf_op jit(solution)/shard_map/concatenate | solution.py:258
  19.0 0.8 %reshape.305.x_ref = bf16[144,1024]{1,0:T(8,128)(2,1)} reshape(bf16[2,6,12,1024]{3,2,1,0:T(8,128)(2,1)S(1)} %fusion.12) | data formatting | bytes 589824 | tf_op jit(solution)/shard_map/reshape | solution.py:145
  19.8 16.9 %shard_map.74 = (bf16[144,1024]{1,0:T(8,128)(2,1)}, bf16[144,1024]{1,0:T(8,128)(2,1)}) custom-call(s32[2,2]{1,0:T(2,128)} %offsets_ref.5, bf16[144,1024]{1,0:T(8,128)(2,1)} %reshape.305.x_ref, bf16[1024,3072]{1,0:T(8,128)(2,1)} %bitcast.14, bf16[1024,3072]{1,0:T(8,128)(2,1)} %bitcast.15, bf16[1024,3072]{1,0:T(8,128)(2,1)} %bitcast.16, ...), custom_call_target="tpu_custom_call" | custom-call | flops 1207959552 | bytes 8388608 | tf_op jit(solution)/shard_map/pallas_call | solution.py:157
  37.3 1.0 %reshape.306 = bf16[2,6,12,1024]{3,2,1,0:T(8,128)(2,1)S(1)} reshape(bf16[144,1024]{1,0:T(8,128)(2,1)} %get-tuple-element.53) | data formatting | bytes 589824 | tf_op jit(solution)/shard_map/reshape | solution.py:325
  38.4 9.0 %conditional.4 = ((bf16[80,1024]{1,0:T(8,128)(2,1)S(1)}, bf16[48,1024]{1,0:T(8,128)(2,1)S(1)}, bf16[80,1024]{1,0:T(8,128)(2,1)S(1)})) conditional(s32[]{:T(128)} %bitcast.6, bf16[2,6,12,1024]{3,2,1,0:T(8,128)(2,1)S(1)} %reshape.306, bf16[2,6,12,1024]{3,2,1,0:T(8,128)(2,1)S(1)} %reshape.306, ...), branch_computations={%region_4.5_spmd, %region_5.6_spmd, %region_6.7_spmd, %region_7.8_... | conditional | bytes 2269198 | solution.py:301
  38.6 0.1 reshape.247
  38.7 8.7 %branch_0_fun.4 = (bf16[80,1024]{1,0:T(8,128)(2,1)S(1)}, bf16[48,1024]{1,0:T(8,128)(2,1)S(1)}, bf16[80,1024]{1,0:T(8,128)(2,1)S(1)}) custom-call(bf16[80,1024]{1,0:T(8,128)(2,1)S(1)} %pad.110.below_in, bf16[48,1024]{1,0:T(8,128)(2,1)S(1)} %pad.111.corner_in, bf16[80,1024]{1,0:T(8,128)(2,1)S(1)} %pad.112.beside_in), custom_call_target="tpu_custom_call" | custom-call | tf_op jit(solution)/shard_map/cond/branch_0_fun/pallas_call | solution.py:222
  47.5 0.8 %fusion.16 = bf16[2,3,12,1024]{3,2,1,0:T(8,128)(2,1)S(1)} fusion(s32[]{:T(128)} %bitcast.7, bf16[2,3,6,1024]{3,2,1,0:T(8,128)(2,1)S(1)} %reshape.372, bf16[2,3,12,1024]{3,2,1,0:T(8,128)(2,1)S(1)} %reshape.371), kind=kLoop, calls=%fused_computation.58 | loop fusion | flops 442368 | bytes 368644 | tf_op jit(solution)/shard_map/concatenate | solution.py:256
  48.3 0.1 reshape.370
  48.4 1.0 %fusion.4 = bf16[2,6,12,1024]{3,2,1,0:T(8,128)(2,1)S(1)} fusion(s32[]{:T(128)} %bitcast.7, bf16[2,6,6,1024]{3,2,1,0:T(8,128)(2,1)S(1)} %reshape.370, bf16[2,6,12,1024]{3,2,1,0:T(8,128)(2,1)S(1)} %reshape.306), kind=kLoop, calls=%fused_computation.35 | loop fusion | flops 884736 | bytes 737284 | tf_op jit(solution)/shard_map/concatenate | solution.py:254
  49.4 0.9 %fusion.10 = bf16[2,6,12,1024]{3,2,1,0:T(8,128)(2,1)S(1)} fusion(s32[]{:T(128)} %bitcast.8, bf16[2,3,12,1024]{3,2,1,0:T(8,128)(2,1)S(1)} %fusion.16, bf16[2,6,12,1024]{3,2,1,0:T(8,128)(2,1)S(1)} %fusion.4), kind=kLoop, calls=%fused_computation.41 | loop fusion | flops 294912 | bytes 737284 | tf_op jit(solution)/shard_map/concatenate | solution.py:258
  50.2 0.8 %reshape.312.x_ref = bf16[144,1024]{1,0:T(8,128)(2,1)} reshape(bf16[2,6,12,1024]{3,2,1,0:T(8,128)(2,1)S(1)} %fusion.10) | data formatting | bytes 589824 | tf_op jit(solution)/shard_map/reshape | solution.py:145
  51.0 0.0 copy-start
  51.0 8.8 %shard_map.75 = bf16[144,1024]{1,0:T(8,128)(2,1)} custom-call(s32[2,2]{1,0:T(2,128)} %offsets_ref.5, bf16[144,1024]{1,0:T(8,128)(2,1)} %reshape.312.x_ref, bf16[1024,3072]{1,0:T(8,128)(2,1)} %bitcast.17, bf16[1024,3072]{1,0:T(8,128)(2,1)} %bitcast.18, bf16[1024,3072]{1,0:T(8,128)(2,1)} %bitcast.19, bf16[1024,1024]{1,0:T(8,128)(2,1)} %bitcast.21, ...), custom_call_target="tpu_custom_call" | custom-call | flops 1207959552 | bytes 8388608 | tf_op jit(solution)/shard_map/pallas_call | solution.py:157
  59.9 0.0 copy-done
  59.9 1.0 %broadcast_select_fusion = bf16[144,1024]{1,0:T(8,128)(2,1)S(1)} fusion(bf16[144,1024]{1,0:T(8,128)(2,1)S(1)} %copy-done, bf16[144,1024]{1,0:T(8,128)(2,1)} %shard_map.75, pred[]{:T(512)S(6)} %eq.27), kind=kLoop, calls=%fused_computation.54 | loop fusion | flops 147456 | bytes 884737 | tf_op jit(solution)/shard_map/jit(_where)/select_n | solution.py:328
  60.9 0.1 reshape.313
  60.9 11.2 %conditional.5 = ((bf16[80,1024]{1,0:T(8,128)(2,1)S(1)}, bf16[48,1024]{1,0:T(8,128)(2,1)S(1)}, bf16[80,1024]{1,0:T(8,128)(2,1)S(1)})) conditional(s32[]{:T(128)} %bitcast, bf16[2,6,12,1024]{3,2,1,0:T(8,128)(2,1)S(1)} %reshape.313, bf16[2,6,12,1024]{3,2,1,0:T(8,128)(2,1)S(1)} %reshape.313, ...), branch_computations={%region_8.9_spmd, %region_9.10_spmd, %region_10.11_spmd, %region_1... | conditional | flops 184324 | bytes 2637882 | solution.py:312
  61.2 0.1 slice_select_fusion.9
  61.3 0.1 reshape.280
  61.4 10.8 %branch_7_fun.1 = (bf16[80,1024]{1,0:T(8,128)(2,1)S(1)}, bf16[48,1024]{1,0:T(8,128)(2,1)S(1)}, bf16[80,1024]{1,0:T(8,128)(2,1)S(1)}) custom-call(bf16[80,1024]{1,0:T(8,128)(2,1)S(1)} %pad.143.below_in, bf16[48,1024]{1,0:T(8,128)(2,1)S(1)} %pad.144.corner_in, bf16[80,1024]{1,0:T(8,128)(2,1)S(1)} %pad.145.beside_in), custom_call_target="tpu_custom_call" | custom-call | tf_op jit(solution)/shard_map/cond/branch_7_fun/pallas_call | solution.py:222
  72.3 0.9 %fusion.14 = bf16[2,3,12,1024]{3,2,1,0:T(8,128)(2,1)S(1)} fusion(s32[]{:T(128)} %bitcast.9, bf16[2,3,6,1024]{3,2,1,0:T(8,128)(2,1)S(1)} %reshape.375, bf16[2,3,12,1024]{3,2,1,0:T(8,128)(2,1)S(1)} %reshape.374), kind=kLoop, calls=%fused_computation.56 | loop fusion | flops 442368 | bytes 368644 | tf_op jit(solution)/shard_map/concatenate | solution.py:256
  73.2 0.1 reshape.373
  73.3 1.1 %fusion.2 = bf16[2,6,12,1024]{3,2,1,0:T(8,128)(2,1)S(1)} fusion(s32[]{:T(128)} %bitcast.9, bf16[2,6,6,1024]{3,2,1,0:T(8,128)(2,1)S(1)} %reshape.373, bf16[2,6,12,1024]{3,2,1,0:T(8,128)(2,1)S(1)} %reshape.313), kind=kLoop, calls=%fused_computation.33 | loop fusion | flops 884736 | bytes 737284 | tf_op jit(solution)/shard_map/concatenate | solution.py:254
  74.4 0.9 %fusion.8 = bf16[2,6,12,1024]{3,2,1,0:T(8,128)(2,1)S(1)} fusion(s32[]{:T(128)} %bitcast.10, bf16[2,3,12,1024]{3,2,1,0:T(8,128)(2,1)S(1)} %fusion.14, bf16[2,6,12,1024]{3,2,1,0:T(8,128)(2,1)S(1)} %fusion.2), kind=kLoop, calls=%fused_computation.39 | loop fusion | flops 294912 | bytes 737284 | tf_op jit(solution)/shard_map/concatenate | solution.py:258
  75.3 1.0 %copy.15 = bf16[2,6,12,1024]{3,0,2,1:T(2,128)(2,1)} copy(bf16[2,6,12,1024]{3,2,1,0:T(8,128)(2,1)S(1)} %fusion.8) | data formatting | bytes 589824 | tf_op jit(solution)/shard_map/dynamic_slice | solution.py:259
  (37 shorter events, 0.8 us)
Async XLA Ops:
  51.0 8.8 %copy-start = (bf16[144,1024]{1,0:T(8,128)(2,1)S(1)}, bf16[144,1024]{1,0:T(8,128)(2,1)}, u32[]{:S(2)}) copy-start(bf16[144,1024]{1,0:T(8,128)(2,1)} %get-tuple-element.51) | copy-start | bytes 884740

commit v6 on v5

--- a/solution.py
+++ b/solution.py
@@ -250,7 +250,7 @@
 
 
 def assembled(field, below, corner, beside, row, column):
-    sliced = functools.partial(lax.dynamic_slice_in_dim, allow_negative_indices=False)
+    sliced = lax.dynamic_slice_in_dim
     near = jnp.concatenate([beside, field, beside], axis=2)
     near = sliced(near, column, field.shape[2], 2)
     far = jnp.concatenate([corner, below, corner], axis=2)

time: 76.9 us -> 82.8 us (1.077)
  between operations: 2.18 us -> 13.4 us
  other arithmetic: 12.1 us -> 6.49 us
    concatenate x3, other arithmetic: 2.64 us -> 0.72 us  [assembled(): tall = jnp.concatenate([far, near, far], axis=1)]
    concatenate x3, other arithmetic: 2.54 us -> 0.7 us  [assembled(): far = jnp.concatenate([corner, below, corner], axis=2)]
    concatenate x3, other arithmetic: 3.18 us -> 1.34 us  [assembled(): near = jnp.concatenate([beside, field, beside], axis=2)]
where the time goes in v6:
time: 82.8 us; the launch traced here: 82 us
  Pallas kernels  56.9 us (69%)
  between operations  13.4 us (16%)
  other arithmetic  6.49 us (8%)
  local copies, waits for them, and re-layouts  4.76 us (6%)
    pallas_call x3, Pallas kernels, exchanged(): pl.pallas_call(functools.partial(exchange_kernel, lat_steps, lon_steps),...  29.9 us
    pallas_call x2, Pallas kernels, attend(): pl.pallas_call(functools.partial(attend_kernel, section, head_size=head_s...  25.7 us

profile of v6, /device:TPU:4, one launch (start us, length us, event | category | flops | bytes accessed | tf_op | source)
XLA Modules:
  0.0 82.0 jit_solution(11600439867716973665)
XLA Ops:
  0.0 1.3 %shard_map.73 = (s32[1]{0:T(128)}, s32[1]{0:T(128)}, s32[1]{0:T(128)}, s32[1]{0:T(128)}, s32[1]{0:T(128)}, /*index=5*/s32[1]{0:T(128)}, s32[1]{0:T(128)}, s32[1]{0:T(128)}, s32[1]{0:T(128)}) custom-call(s32[2,2]{1,0:T(2,128)} %offsets_ref.5), custom_call_target="tpu_custom_call" | custom-call | tf_op jit(solution)/shard_map/pallas_call | solution.py:289
  10.3 0.7 convert_element_type.73
  10.9 0.7 broadcast_compare_fusion
  11.6 1.2 %fusion = bf16[2,6,12,1024]{3,2,1,0:T(8,128)(2,1)S(1)} fusion(bf16[2,6,12,1024]{3,0,2,1:T(2,128)(2,1)} %param.23, f32[1024]{0:T(1024)S(1)} %convert_element_type.73, pred[6,12]{1,0:T(8,128)(4,1)S(1)} %broadcast_compare_fusion), kind=kLoop, calls=%fused_computation.13 | loop fusion | flops 589824 | bytes 593992 | tf_op jit(solution)/shard_map/convert_element_type | solution.py:319
  12.9 10.8 %conditional.3 = ((bf16[80,1024]{1,0:T(8,128)(2,1)S(1)}, bf16[48,1024]{1,0:T(8,128)(2,1)S(1)}, bf16[80,1024]{1,0:T(8,128)(2,1)S(1)})) conditional(s32[]{:T(128)} %bitcast.1, bf16[2,6,12,1024]{3,2,1,0:T(8,128)(2,1)S(1)} %fusion, bf16[2,6,12,1024]{3,2,1,0:T(8,128)(2,1)S(1)} %fusion, ...), branch_computations={%region_0.1_spmd, %region_1.2_spmd, %region_2.3_spmd, %region_3.4_... | conditional | bytes 2269198 | solution.py:301
  13.1 0.1 slice.202
  13.1 0.1 reshape.244
  13.2 10.4 %branch_3_fun.3 = (bf16[80,1024]{1,0:T(8,128)(2,1)S(1)}, bf16[48,1024]{1,0:T(8,128)(2,1)S(1)}, bf16[80,1024]{1,0:T(8,128)(2,1)S(1)}) custom-call(bf16[80,1024]{1,0:T(8,128)(2,1)S(1)} %pad.107.below_in, bf16[48,1024]{1,0:T(8,128)(2,1)S(1)} %pad.108.corner_in, bf16[80,1024]{1,0:T(8,128)(2,1)S(1)} %pad.109.beside_in), custom_call_target="tpu_custom_call" | custom-call | tf_op jit(solution)/shard_map/cond/branch_3_fun/pallas_call | solution.py:222
  23.8 0.2 fusion.18
  24.0 0.1 reshape.367
  24.1 0.4 fusion.6
  24.5 0.2 fusion.12
  24.8 0.8 reshape.305.x_ref
  25.6 16.9 %shard_map.74 = (bf16[144,1024]{1,0:T(8,128)(2,1)}, bf16[144,1024]{1,0:T(8,128)(2,1)}) custom-call(s32[2,2]{1,0:T(2,128)} %offsets_ref.5, bf16[144,1024]{1,0:T(8,128)(2,1)} %reshape.305.x_ref, bf16[1024,3072]{1,0:T(8,128)(2,1)} %bitcast.14, bf16[1024,3072]{1,0:T(8,128)(2,1)} %bitcast.15, bf16[1024,3072]{1,0:T(8,128)(2,1)} %bitcast.16, ...), custom_call_target="tpu_custom_call" | custom-call | flops 1207959552 | bytes 8388608 | tf_op jit(solution)/shard_map/pallas_call | solution.py:157
  46.7 1.0 %reshape.306 = bf16[2,6,12,1024]{3,2,1,0:T(8,128)(2,1)S(1)} reshape(bf16[144,1024]{1,0:T(8,128)(2,1)} %get-tuple-element.53) | data formatting | bytes 589824 | tf_op jit(solution)/shard_map/reshape | solution.py:325
  47.7 9.0 %conditional.4 = ((bf16[80,1024]{1,0:T(8,128)(2,1)S(1)}, bf16[48,1024]{1,0:T(8,128)(2,1)S(1)}, bf16[80,1024]{1,0:T(8,128)(2,1)S(1)})) conditional(s32[]{:T(128)} %bitcast.6, bf16[2,6,12,1024]{3,2,1,0:T(8,128)(2,1)S(1)} %reshape.306, bf16[2,6,12,1024]{3,2,1,0:T(8,128)(2,1)S(1)} %reshape.306, ...), branch_computations={%region_4.5_spmd, %region_5.6_spmd, %region_6.7_spmd, %region_7.8_... | conditional | bytes 2269198 | solution.py:301
  47.9 0.1 reshape.247
  48.0 8.7 %branch_0_fun.4 = (bf16[80,1024]{1,0:T(8,128)(2,1)S(1)}, bf16[48,1024]{1,0:T(8,128)(2,1)S(1)}, bf16[80,1024]{1,0:T(8,128)(2,1)S(1)}) custom-call(bf16[80,1024]{1,0:T(8,128)(2,1)S(1)} %pad.110.below_in, bf16[48,1024]{1,0:T(8,128)(2,1)S(1)} %pad.111.corner_in, bf16[80,1024]{1,0:T(8,128)(2,1)S(1)} %pad.112.beside_in), custom_call_target="tpu_custom_call" | custom-call | tf_op jit(solution)/shard_map/cond/branch_0_fun/pallas_call | solution.py:222
  56.8 0.2 fusion.16
  57.1 0.1 reshape.370
  57.2 0.4 fusion.4
  57.6 0.2 fusion.10
  57.9 0.8 reshape.312.x_ref
  58.6 0.0 copy-start
  58.7 8.8 %shard_map.75 = bf16[144,1024]{1,0:T(8,128)(2,1)} custom-call(s32[2,2]{1,0:T(2,128)} %offsets_ref.5, bf16[144,1024]{1,0:T(8,128)(2,1)} %reshape.312.x_ref, bf16[1024,3072]{1,0:T(8,128)(2,1)} %bitcast.17, bf16[1024,3072]{1,0:T(8,128)(2,1)} %bitcast.18, bf16[1024,3072]{1,0:T(8,128)(2,1)} %bitcast.19, bf16[1024,1024]{1,0:T(8,128)(2,1)} %bitcast.21, ...), custom_call_target="tpu_custom_call" | custom-call | flops 1207959552 | bytes 8388608 | tf_op jit(solution)/shard_map/pallas_call | solution.py:157
  67.5 0.0 copy-done
  67.5 1.0 %broadcast_select_fusion = bf16[144,1024]{1,0:T(8,128)(2,1)S(1)} fusion(bf16[144,1024]{1,0:T(8,128)(2,1)S(1)} %copy-done, bf16[144,1024]{1,0:T(8,128)(2,1)} %shard_map.75, pred[]{:T(512)S(6)} %eq.27), kind=kLoop, calls=%fused_computation.54 | loop fusion | flops 147456 | bytes 884737 | tf_op jit(solution)/shard_map/jit(_where)/select_n | solution.py:328
  68.5 0.1 reshape.313
  68.6 11.2 %conditional.5 = ((bf16[80,1024]{1,0:T(8,128)(2,1)S(1)}, bf16[48,1024]{1,0:T(8,128)(2,1)S(1)}, bf16[80,1024]{1,0:T(8,128)(2,1)S(1)})) conditional(s32[]{:T(128)} %bitcast, bf16[2,6,12,1024]{3,2,1,0:T(8,128)(2,1)S(1)} %reshape.313, bf16[2,6,12,1024]{3,2,1,0:T(8,128)(2,1)S(1)} %reshape.313, ...), branch_computations={%region_8.9_spmd, %region_9.10_spmd, %region_10.11_spmd, %region_1... | conditional | flops 184324 | bytes 2637882 | solution.py:312
  68.8 0.1 slice_select_fusion.9
  68.9 0.1 reshape.280
  69.0 10.8 %branch_7_fun.1 = (bf16[80,1024]{1,0:T(8,128)(2,1)S(1)}, bf16[48,1024]{1,0:T(8,128)(2,1)S(1)}, bf16[80,1024]{1,0:T(8,128)(2,1)S(1)}) custom-call(bf16[80,1024]{1,0:T(8,128)(2,1)S(1)} %pad.143.below_in, bf16[48,1024]{1,0:T(8,128)(2,1)S(1)} %pad.144.corner_in, bf16[80,1024]{1,0:T(8,128)(2,1)S(1)} %pad.145.beside_in), custom_call_target="tpu_custom_call" | custom-call | tf_op jit(solution)/shard_map/cond/branch_7_fun/pallas_call | solution.py:222
  79.9 0.2 fusion.14
  80.2 0.1 reshape.373
  80.3 0.4 fusion.2
  80.7 0.2 fusion.8
  80.9 1.0 %copy.15 = bf16[2,6,12,1024]{3,0,2,1:T(2,128)(2,1)} copy(bf16[2,6,12,1024]{3,2,1,0:T(8,128)(2,1)S(1)} %fusion.8) | data formatting | bytes 589824 | tf_op jit(solution)/shard_map/dynamic_slice | solution.py:259
  (37 shorter events, 0.8 us)
Async XLA Ops:
  58.6 8.9 %copy-start = (bf16[144,1024]{1,0:T(8,128)(2,1)S(1)}, bf16[144,1024]{1,0:T(8,128)(2,1)}, u32[]{:S(2)}) copy-start(bf16[144,1024]{1,0:T(8,128)(2,1)} %get-tuple-element.51) | copy-start | bytes 884740
